TPU v7x, 32 devices: a whole 2x2x4 slice. The times are simulated.
32 devices in a mesh: dp: 8 (over z, x), ctx: 4 (over y, core).
Axes of the slice: x: 2, y: 2, z: 4, core: 2. Of those that a mesh axis runs over, the one named last changes fastest.
Arguments:
- tokens: bfloat16 [2, 16384, 576], P(None, ('dp', 'ctx')), may hold values from -6 to 6
- lengths: int32 [2, 8, 4], P(None, 'dp'), may hold values from 1 to 2045, as said below
- weights: float32 [3538944], P(('dp', 'ctx'))
- momentum: float32 [3538944], P(('dp', 'ctx'))
- norm_gains: float32 [2, 576], replicated, may hold values from 0.5 to 1.5
- gain_first: float32 [2, 576], replicated, may hold values from -57.926186 to 57.926186
- gain_second: float32 [2, 576], replicated, may hold values from 425.984 to 6553.6
- cotangent: bfloat16 [2, 16384, 576], P(None, ('dp', 'ctx')), may hold values from -12 to 12
Outputs:
- outputs: float32 [2, 16384, 576], P(None, ('dp', 'ctx'))
- d_tokens: float32 [2, 16384, 576], P(None, ('dp', 'ctx'))
- weight_grads: float32 [3538944], P(('dp', 'ctx'))
- new_momentum: float32 [3538944], P(('dp', 'ctx'))
- new_weights: float32 [3538944], P(('dp', 'ctx'))
- gain_first_new: float32 [2, 576], replicated
- gain_second_new: float32 [2, 576], replicated
- new_gains: float32 [2, 576], replicated
Inputs may be any that keep to these rules, and one draw needn't show every extreme that they name: Each row of lengths sums to 2048; its entry 1 equals 2048 minus the other three, and each other entry lies between 1 and 255. In every draw one buffer has all three other entries equal to 1.
All inputs are finite; a program needn't handle non-finite values.
Results may differ from a plain program's by a relative error of at most 0.015.
Values may be sent and summed in bfloat16 or wider, within the bound.
No kernel may reach another device: no remote copies, remote signals or barrier semaphores. Data moves between devices by JAX's collectives and lax.ppermute only.
A program may use at most 384 MiB of HBM per device.

v0:
```python
from functools import partial
import math

import jax
import jax.numpy as jnp
from jax import lax
from jax.experimental import pallas as pl
from jax.experimental.pallas import tpu as pltpu
from jax.sharding import Mesh, PartitionSpec as P

HEADS = 9
KV_HEADS = 3
HEAD_DIM = 64
FF = 1536
NS_STEPS = 5
ADAM_STEP = 10
D = 576
KV_WIDTH = 192
GROUPS = HEADS // KV_HEADS
TOK = 512
TILE = 256
COLS = GROUPS * TILE
ROW_CUT = 4
COL_CUT = 2
CHUNKS = ROW_CUT * COL_CUT
CHUNK_ROWS = D // ROW_CUT
CHUNK_COLS = FF // COL_CUT
PLANE = ("half", "ctx")
EVERY = ("quarter", "rep", "half", "ctx")


norm_epsilon = 1e-05
rope_base = 100000.0
masked_score = -1e30
newton_first = 3.4445
newton_second = -4.775
newton_third = 2.0315
momentum_decay = 0.95
matrix_rate = 0.2
weight_decay = 0.1
gain_rate = 0.2
first_decay = 0.9
second_decay = 0.95
adam_epsilon = 1e-08
frobenius_epsilon = 1e-07


def layout(lengths_row, places):
    finish = jnp.cumsum(lengths_row)
    firsts = finish - lengths_row
    begins = jnp.max(jnp.where(places[:, None] >= firsts[None, :], firsts[None, :], 0), axis=1)
    return (places - begins, begins)


def rope_tables(offsets):
    half_width = HEAD_DIM // 2
    inverse = jnp.exp(
        jnp.arange(half_width, dtype=jnp.float32) * (-2.0 * math.log(rope_base) / HEAD_DIM)
    )
    angles = inverse[:, None] * offsets.astype(jnp.float32)[None, :]
    return (jnp.cos(angles), jnp.sin(angles))


def dot32(left, right):
    return jnp.dot(left, right, preferred_element_type=jnp.float32)


def masked(scores, key_block, begins, places):
    keys = key_block * TILE + lax.broadcasted_iota(jnp.int32, scores.shape, 0)
    return jnp.where((keys >= begins) & (keys <= places), scores, masked_score)


def tile_row(row, tile):
    part = row[:, tile * TILE : (tile + 1) * TILE]
    return jnp.concatenate([part] * GROUPS, axis=1)


def tile_heads(ref, group, tile):
    return jnp.concatenate(
        [ref[group, head, :, tile * TILE : (tile + 1) * TILE] for head in range(GROUPS)], axis=1
    )


def positions():
    ctx = lax.axis_index("ctx")
    return (lax.axis_index("quarter"), lax.axis_index("half"), lax.div(ctx, 2), lax.rem(ctx, 2))


def chunk_spot():
    _, half, chip, core = positions()
    return core * 4 + half * 2 + chip


def first_key(lengths_ref, slot, row):
    micro = slot ^ positions()[2]
    begin = jnp.int32(0)
    first = jnp.int32(0)
    for place in range(3):
        first = first + lengths_ref[micro, place]
        begin = jnp.where(row >= first, first, begin)
    return begin


def key_loop(lengths_ref, slot, own, tile, load, process, carry):
    last = own * (TOK // TILE) + tile
    first = lax.div(first_key(lengths_ref, slot, last * TILE), TILE)
    full = lax.div(first_key(lengths_ref, slot, last * TILE + TILE - 1) + TILE - 1, TILE)
    full = jnp.minimum(full, last)
    pairs = lax.div(last - full, 2)

    def alone(block, held):
        load(0, block)
        return process(0, True, block, held)

    def couple(pair, held):
        block = full + 2 * pair
        load(1, block + 1)
        held = process(0, False, block, held)
        load(0, block + 2)
        return process(1, False, block + 1, held)

    def single(block, held):
        held = process(0, False, block, held)
        load(0, last)
        return held

    carry = lax.fori_loop(first, full, alone, carry)
    load(0, full)
    carry = lax.fori_loop(0, pairs, couple, carry)
    carry = lax.fori_loop(full + 2 * pairs, last, single, carry)
    return process(0, True, last, carry)


def plain_key_loop(lengths_ref, micro, own, tile, step, carry):
    last = own * (TOK // TILE) + tile
    first = lax.div(first_key(lengths_ref, micro, last * TILE), TILE)
    full = lax.div(first_key(lengths_ref, micro, last * TILE + TILE - 1) + TILE - 1, TILE)
    full = jnp.minimum(full, last)
    pairs = lax.div(last - full, 2)
    carry = lax.fori_loop(first, full, partial(step, True, 1), carry)
    carry = lax.fori_loop(
        0, pairs, lambda pair, held: step(False, 2, full + 2 * pair, held), carry
    )
    carry = lax.fori_loop(full + 2 * pairs, last, partial(step, False, 1), carry)
    return step(True, 1, last, carry)


def key_rows(block):
    return pl.ds(pl.multiple_of(block * TILE, TILE), TILE)


def own_block(slot):
    ctx = lax.axis_index("ctx")
    return jnp.maximum(ctx, 3 - ctx) if slot else jnp.minimum(ctx, 3 - ctx)


def key_slots(own, micro, kv_ref, other_ref, far_ref, far_other_ref):
    refs = (kv_ref.at[micro], other_ref.at[micro], far_ref, far_other_ref)[: 2 + 2 * micro]
    return [(own ^ place, ref) for place, ref in enumerate(refs)]


def block_rows(block):
    return pl.ds(pl.multiple_of(block * TOK, TOK), TOK)


def forward_kernel(
    micro, lengths_ref, q_ref, kv_ref, other_ref, far_ref, far_other_ref, begin_ref, tie_ref,
    o_ref, lse_ref, k_nat, v_ext, s_ref, p_ref,
):
    own = own_block(micro)
    for block, source in key_slots(own, micro, kv_ref, other_ref, far_ref, far_other_ref):

        @pl.when(block <= own)
        def _():
            rows = block_rows(block)
            for group in range(KV_HEADS):
                low = HEAD_DIM * group
                k_nat[group, rows, :] = source[low : low + HEAD_DIM, :].T
                low = low + KV_WIDTH
                v_ext[group, :HEAD_DIM, rows] = source[low : low + HEAD_DIM, :]
                v_ext[group, HEAD_DIM:, rows] = jnp.ones((16, TOK), jnp.bfloat16)

    def one_group(group, unused):
        for tile in range(TOK // TILE):
            queries = tile_heads(q_ref, group, tile)
            begins = tile_row(begin_ref[...], tile)
            column = lax.broadcasted_iota(jnp.int32, (1, COLS), 1)
            places = own * TOK + tile * TILE + lax.rem(column, TILE)

            def load(side, block):
                s_ref[side] = dot32(k_nat[group, key_rows(block), :], queries)

            def process(side, is_masked, block, carry):
                top, total = carry
                scores_ref, probs_ref = s_ref.at[side], p_ref.at[side]
                if is_masked:
                    scores_ref[...] = masked(scores_ref[...], block, begins, places)
                highest = scores_ref[:16]
                for low in range(16, TILE, 16):
                    highest = jnp.maximum(highest, scores_ref[low : low + 16])
                new_top = jnp.maximum(top, jnp.max(highest, axis=0, keepdims=True))
                for low in range(0, TILE, 16):
                    rows = slice(low, low + 16)
                    probs_ref[rows] = jnp.exp(scores_ref[rows] - new_top).astype(jnp.bfloat16)
                total = total * jnp.exp(top - new_top) + dot32(
                    v_ext[group, :, key_rows(block)], probs_ref[...]
                )
                return (new_top, total)

            carry = (
                jnp.full((1, COLS), masked_score, jnp.float32),
                jnp.zeros((HEAD_DIM + 16, COLS), jnp.float32),
            )
            top, total = key_loop(lengths_ref, micro, own, tile, load, process, carry)
            weight = total[HEAD_DIM : HEAD_DIM + 1, :]
            mixed = (total[:HEAD_DIM, :] / weight).astype(jnp.bfloat16)
            log_total = top + jnp.log(weight)
            for head in range(GROUPS):
                o_ref[group, head, :, tile * TILE : (tile + 1) * TILE] = mixed[
                    :, head * TILE : (head + 1) * TILE
                ]
                lse_ref[group, head, :, tile * TILE : (tile + 1) * TILE] = log_total[
                    :, head * TILE : (head + 1) * TILE
                ]
        return unused

    lax.fori_loop(0, KV_HEADS, one_group, 0)


def backward_kernel(
    micro, lengths_ref, q_ref, kv_ref, other_ref, far_ref, far_other_ref, begin_ref, o_ref, lse_ref,
    do_ref, cos_ref, sin_ref, tie_ref,
    dq_ref, keep_ref, send_ref, k_nat, v_nat, k_tall, dk_ref, dv_ref, s_ref, g_ref, p_ref, ds_ref,
):
    own = own_block(micro)
    slots = key_slots(own, micro, kv_ref, other_ref, far_ref, far_other_ref)
    for block, source in slots:

        @pl.when(block <= own)
        def _():
            rows = block_rows(block)
            for group in range(KV_HEADS):
                low = HEAD_DIM * group
                k_nat[group, rows, :] = source[low : low + HEAD_DIM, :].T
                k_tall[group, :, rows] = source[low : low + HEAD_DIM, :]
                low = low + KV_WIDTH
                v_nat[group, rows, :] = source[low : low + HEAD_DIM, :].T
                dk_ref[group, rows, :] = jnp.zeros((TOK, HEAD_DIM), jnp.float32)
                dv_ref[group, rows, :] = jnp.zeros((TOK, HEAD_DIM), jnp.float32)

    def one_group(group, unused):
        for tile in range(TOK // TILE):
            queries = tile_heads(q_ref, group, tile)
            upstream = tile_heads(do_ref, group, tile)
            mixed = tile_heads(o_ref, group, tile)
            log_total = tile_heads(lse_ref, group, tile)
            delta = jnp.sum(
                upstream.astype(jnp.float32) * mixed.astype(jnp.float32), axis=0, keepdims=True
            )
            queries_nat = queries.T
            upstream_nat = upstream.T
            begins = tile_row(begin_ref[...], tile)
            column = lax.broadcasted_iota(jnp.int32, (1, COLS), 1)
            places = own * TOK + tile * TILE + lax.rem(column, TILE)

            def step(is_masked, width, key_block, dq):
                rows = pl.ds(pl.multiple_of(key_block * TILE, TILE), width * TILE)
                count = width * TILE
                scores = dot32(k_nat[group, rows, :], queries)
                s_ref[:count] = masked(scores, key_block, begins, places) if is_masked else scores
                g_ref[:count] = dot32(v_nat[group, rows, :], upstream)
                for low in range(0, count, 16):
                    part = slice(low, low + 16)
                    probs = jnp.exp(s_ref[part] - log_total)
                    p_ref[part] = probs.astype(jnp.bfloat16)
                    ds_ref[part] = (probs * (g_ref[part] - delta)).astype(jnp.bfloat16)
                dv_ref[group, rows, :] += dot32(p_ref[:count], upstream_nat)
                dk_ref[group, rows, :] += dot32(ds_ref[:count], queries_nat)
                return dq + dot32(k_tall[group, :, rows], ds_ref[:count])

            dq = jnp.zeros((HEAD_DIM, COLS), jnp.float32)
            dq = plain_key_loop(lengths_ref, micro, own, tile, step, dq) * 0.125
            half_width = HEAD_DIM // 2
            cosine = tile_row(cos_ref[...], tile)
            sine = tile_row(sin_ref[...], tile)
            former, latter = dq[:half_width], dq[half_width:]
            turned = jnp.concatenate(
                [former * cosine + latter * sine, latter * cosine - former * sine], axis=0
            ).astype(jnp.bfloat16)
            for head in range(GROUPS):
                dq_ref[group, head, :, tile * TILE : (tile + 1) * TILE] = turned[
                    :, head * TILE : (head + 1) * TILE
                ]
        return unused

    lax.fori_loop(0, KV_HEADS, one_group, 0)
    for place, (block, _) in enumerate(slots):
        out_ref = (keep_ref, send_ref)[place % 2]

        @pl.when(block <= own)
        def _():
            rows = block_rows(block)
            for group in range(KV_HEADS):
                low = HEAD_DIM * group
                out_ref[place // 2, low : low + HEAD_DIM, :] = dk_ref[group, rows, :].T.astype(
                    jnp.bfloat16
                )
                low = low + KV_WIDTH
                out_ref[place // 2, low : low + HEAD_DIM, :] = dv_ref[group, rows, :].T.astype(
                    jnp.bfloat16
                )

        @pl.when(block > own)
        def _():
            out_ref[place // 2] = jnp.zeros((2 * KV_WIDTH, TOK), jnp.bfloat16)


def vmem():
    return pl.BlockSpec(memory_space=pltpu.VMEM)


def smem():
    return pl.BlockSpec(memory_space=pltpu.SMEM)


def anywhere():
    return pl.BlockSpec(memory_space=pl.ANY)


kernel_params = pltpu.CompilerParams(vmem_limit_bytes=56 * 1024 * 1024)
heads_shape = (KV_HEADS, GROUPS, HEAD_DIM, TOK)


def attend_forward(micro, lengths, queries, keyvals, begins, tie):
    return pl.pallas_call(
        partial(forward_kernel, micro),
        out_shape=(
            jax.ShapeDtypeStruct(heads_shape, jnp.bfloat16),
            jax.ShapeDtypeStruct((KV_HEADS, GROUPS, 1, TOK), jnp.float32),
        ),
        in_specs=[smem()] + [vmem()] * 6 + [anywhere()],
        out_specs=(vmem(), vmem()),
        scratch_shapes=[
            pltpu.VMEM((KV_HEADS, 4 * TOK, HEAD_DIM), jnp.bfloat16),
            pltpu.VMEM((KV_HEADS, HEAD_DIM + 16, 4 * TOK), jnp.bfloat16),
            pltpu.VMEM((2, TILE, COLS), jnp.float32),
            pltpu.VMEM((2, TILE, COLS), jnp.bfloat16),
        ],
        compiler_params=kernel_params,
        cost_estimate=pl.CostEstimate(
            flops=4 * 9 * 64 * TOK * 2048, bytes_accessed=4000000, transcendentals=9 * TOK * 2048
        ),
        name="attend_forward",
    )(lengths, queries, *keyvals, begins, tie)


def attend_back(
    micro, lengths, queries, keyvals, begins, mixed, log_total, grad_mixed, cosine, sine, tie
):
    half_shape = (1 + micro, 2 * KV_WIDTH, TOK)
    return pl.pallas_call(
        partial(backward_kernel, micro),
        out_shape=(
            jax.ShapeDtypeStruct(heads_shape, jnp.bfloat16),
            jax.ShapeDtypeStruct(half_shape, jnp.bfloat16),
            jax.ShapeDtypeStruct(half_shape, jnp.bfloat16),
        ),
        in_specs=[smem()] + [vmem()] * 11 + [anywhere()],
        out_specs=(vmem(),) * 3,
        scratch_shapes=[
            pltpu.VMEM((KV_HEADS, 4 * TOK, HEAD_DIM), jnp.bfloat16),
            pltpu.VMEM((KV_HEADS, 4 * TOK, HEAD_DIM), jnp.bfloat16),
            pltpu.VMEM((KV_HEADS, HEAD_DIM, 4 * TOK), jnp.bfloat16),
            pltpu.VMEM((KV_HEADS, 4 * TOK, HEAD_DIM), jnp.float32),
            pltpu.VMEM((KV_HEADS, 4 * TOK, HEAD_DIM), jnp.float32),
            pltpu.VMEM((2 * TILE, COLS), jnp.float32),
            pltpu.VMEM((2 * TILE, COLS), jnp.float32),
            pltpu.VMEM((2 * TILE, COLS), jnp.bfloat16),
            pltpu.VMEM((2 * TILE, COLS), jnp.bfloat16),
        ],
        compiler_params=kernel_params,
        cost_estimate=pl.CostEstimate(
            flops=10 * 9 * 64 * TOK * 2048, bytes_accessed=8000000, transcendentals=9 * TOK * 2048
        ),
        name="attend_back",
    )(lengths, queries, *keyvals, begins, mixed, log_total, grad_mixed, cosine, sine, tie)


def dot_with(left, right, left_side, right_side):
    return lax.dot_general(
        left, right, (((left_side,), (right_side,)), ((), ())), preferred_element_type=jnp.float32
    )


def norm_back(values, scaling, gain, upstream, axis):
    weighted = upstream * gain
    inner = jnp.mean(weighted * values, axis=axis, keepdims=True)
    gain_grad = jnp.sum(upstream * values * scaling, axis=1 - axis, keepdims=True)
    return (scaling * weighted - values * (scaling * scaling * scaling) * inner, gain_grad)


def norm_scaling(values, axis):
    return lax.rsqrt(jnp.mean(values * values, axis=axis, keepdims=True) + norm_epsilon)


def row_parts(held, spot, side):
    for turn in range(ROW_CUT):
        start = (turn ^ lax.div(spot, COL_CUT)) * CHUNK_ROWS
        part = held[pl.ds(pl.multiple_of(start, CHUNK_ROWS), CHUNK_ROWS), :]
        yield (turn * COL_CUT + side, part.astype(jnp.bfloat16))


def store_result(slot, result, out_ref, moved_ref):
    chip = positions()[2]

    @pl.when(chip == slot)
    def _():
        out_ref[0] = result

    @pl.when(chip != slot)
    def _():
        moved_ref[...] = result.astype(jnp.bfloat16)


def mlp_kernel(
    x_ref, x1_ref, c_ref, c1_ref, o0_ref, o1_ref, wo_ref, w_ref, wd_ref, gain_ref,
    out_ref, out1_ref, dh_ref, do0_ref, do1_ref, keep_ref, send_ref, gwo_ref, gg_ref,
    hid, dgate, dup, n2_tall, dh_low, held, gate_ref, up_ref, da_ref, c_slots,
):
    gain = gain_ref[...]
    gg_ref[...] = jnp.zeros((1, D), jnp.float32)
    block = 256
    spot = chunk_spot()
    for micro, (o_ref, do_ref) in enumerate(((o0_ref, do0_ref), (o1_ref, do1_ref))):
        rows = slice(micro * TOK, (micro + 1) * TOK)
        x_tall = (x1_ref if micro else x_ref)[...]
        c_tall_ref = c_slots.at[micro]
        chip = positions()[2]

        @pl.when(chip == micro)
        def _():
            c_tall_ref[...] = c_ref[0]

        @pl.when(chip != micro)
        def _():
            c_tall_ref[...] = c1_ref[...]

        c_tall = c_tall_ref[...]
        hidden_state = (x_tall.astype(jnp.float32) + dot_with(wo_ref[...], o_ref[...], 0, 0)).T
        scaling = norm_scaling(hidden_state, 1)
        normed = (hidden_state * scaling * gain).astype(jnp.bfloat16)
        n2_tall[:, rows] = normed.T
        back = c_tall.T
        for column in range(0, FF, block):
            columns = slice(column, column + block)
            gate_ref[...] = dot32(normed, w_ref[:, columns])
            up_ref[...] = dot32(normed, w_ref[:, FF + column : FF + column + block])
            da_ref[...] = dot_with(back, wd_ref[columns, :], 1, 1)
            for low in range(0, TOK, 32):
                part, spot_rows = slice(low, low + 32), slice(micro * TOK + low, micro * TOK + low + 32)
                gate, upward, grad_hidden = gate_ref[part], up_ref[part], da_ref[part]
                sigmoid_gate = jax.nn.sigmoid(gate)
                activated = gate * sigmoid_gate
                hid[spot_rows, columns] = (activated * upward).astype(jnp.bfloat16)
                dup[spot_rows, columns] = (grad_hidden * activated).astype(jnp.bfloat16)
                slope = sigmoid_gate * (1.0 + gate * (1.0 - sigmoid_gate))
                dgate[spot_rows, columns] = (grad_hidden * upward * slope).astype(jnp.bfloat16)
        result = (hidden_state + dot32(hid[rows, :], wd_ref[...])).T
        store_result(micro, result, out_ref, out1_ref)
        upstream = dot_with(dgate[rows, :], w_ref[:, :FF], 1, 1) + dot_with(
            dup[rows, :], w_ref[:, FF:], 1, 1
        )
        part, gain_grad = norm_back(hidden_state, scaling, gain, upstream, 1)
        gg_ref[...] += gain_grad
        grad_state = back.astype(jnp.float32) + part
        dh_low[rows, :] = grad_state.astype(jnp.bfloat16)
        grad_tall = grad_state.T
        dh_ref[micro] = grad_tall
        do_ref[...] = dot32(wo_ref[...], grad_tall.astype(jnp.bfloat16)).astype(jnp.bfloat16)
    c_parts = (c_slots.at[0], c_slots.at[1])
    for place, right in enumerate((dgate, dup, hid)):
        for side in range(COL_CUT):
            start = (side ^ lax.rem(spot, COL_CUT)) * CHUNK_COLS
            for column in range(0, CHUNK_COLS, block):
                columns = pl.ds(pl.multiple_of(start + column, block), block)
                if place < 2:
                    held[...] = dot32(n2_tall[...], right[:, columns])
                else:
                    held[...] = dot32(c_parts[0][...], right[:TOK, columns]) + dot32(
                        c_parts[1][...], right[TOK:, columns]
                    )
                for index, part in row_parts(held, spot, side):
                    out = (keep_ref, send_ref)[index // 4]
                    out[index % 4, place, :, column : column + block] = part
    gwo_ref[...] = (
        dot32(o0_ref[...], dh_low[:TOK, :]) + dot32(o1_ref[...], dh_low[TOK:, :])
    ).astype(jnp.bfloat16)


def mlp(tokens, tokens_1, cotangent, cotangent_1, mixed, w_out, w_gate_up, w_down, gain):
    rows = 2 * TOK
    low = jnp.bfloat16
    chunk_shape = (CHUNKS // 2, 3, CHUNK_ROWS, CHUNK_COLS)
    return pl.pallas_call(
        mlp_kernel,
        out_shape=(
            jax.ShapeDtypeStruct((2, D, TOK), jnp.float32),
            jax.ShapeDtypeStruct((D, TOK), low),
            jax.ShapeDtypeStruct((2, D, TOK), jnp.float32),
            jax.ShapeDtypeStruct((D, TOK), low),
            jax.ShapeDtypeStruct((D, TOK), low),
            jax.ShapeDtypeStruct(chunk_shape, low),
            jax.ShapeDtypeStruct(chunk_shape, low),
            jax.ShapeDtypeStruct((D, D), low),
            jax.ShapeDtypeStruct((1, D), jnp.float32),
        ),
        in_specs=[vmem()] * 10,
        out_specs=(vmem(),) * 9,
        scratch_shapes=[
            pltpu.VMEM((rows, FF), low),
            pltpu.VMEM((rows, FF), low),
            pltpu.VMEM((rows, FF), low),
            pltpu.VMEM((D, rows), low),
            pltpu.VMEM((rows, D), low),
            pltpu.VMEM((D, 256), jnp.float32),
            pltpu.VMEM((TOK, 256), jnp.float32),
            pltpu.VMEM((TOK, 256), jnp.float32),
            pltpu.VMEM((TOK, 256), jnp.float32),
            pltpu.VMEM((2, D, TOK), low),
        ],
        compiler_params=kernel_params,
        cost_estimate=pl.CostEstimate(
            flops=6 * rows * 3 * D * FF, bytes_accessed=25000000, transcendentals=rows * FF
        ),
        name="mlp",
    )(tokens, tokens_1, cotangent, cotangent_1, *mixed, w_out, w_gate_up, w_down, gain)


def natural_tiles(flat, base, rows, width):
    pairs, step, whole = rows // 2, width * 2 // 128, width // 128
    parts = [flat[pl.ds(base + place, pairs, stride=step), :] for place in range(step)]
    even = parts[:whole] + [parts[whole][:, :HEAD_DIM]]
    odd = jnp.concatenate([parts[whole][:, HEAD_DIM:]] + parts[whole + 1 :], axis=1)
    return even, [odd[:, low : low + 128] for low in range(0, width, 128)]


def unflatten(flat, base, rows, width, tiles):
    even, odd = natural_tiles(flat, base, rows, width)
    for place, (first, second) in enumerate(zip(even, odd)):
        breadth = first.shape[1]
        if breadth < 128:
            blank = jnp.zeros((rows // 2, 128 - breadth), jnp.float32)
            first = jnp.concatenate([first, blank], axis=1)
            second = jnp.concatenate([second, blank], axis=1)
        tiles[place, pl.ds(0, rows // 2, stride=2), :] = first
        tiles[place, pl.ds(1, rows // 2, stride=2), :] = second


def tile_widths(width):
    return [(place, low, min(128, width - low)) for place, low in enumerate(range(0, width, 128))]


MIXED = ((0, 0, D), (2592, D, KV_WIDTH), (3456, D + KV_WIDTH, KV_WIDTH), (4320, FF - D, D))


def project_kernel(
    near_ref, next_ref, x_ref, x1_ref, gain_ref, cos0_ref, sin0_ref, cos1_ref, sin1_ref,
    q0_ref, q1_ref, kv_ref, w_ref, wo_ref, n_ref, flat, tiles,
):
    spot = chunk_spot()
    length = flat.shape[0] // CHUNKS
    for index in range(CHUNKS):
        chunk = spot ^ index
        core, half, chip = lax.div(chunk, 4), lax.rem(lax.div(chunk, 2), 2), lax.rem(chunk, 2)
        start = pl.multiple_of((half * 4 + chip * 2 + core) * length, 8)
        part = (near_ref, next_ref)[index // 4][index % 4]
        flat[pl.ds(start, length), :] = part.astype(jnp.float32)
    for base, start, width in MIXED:
        unflatten(flat, base, D, width, tiles)
        for place, low, breadth in tile_widths(width):
            part = tiles[place][:D, :breadth].astype(jnp.bfloat16)
            if start < FF - D:
                w_ref[:, start + low : start + low + breadth] = part
            else:
                wo_ref[:, low : low + breadth] = part
    tall = w_ref[...].T
    half_width = HEAD_DIM // 2
    tables = ((q0_ref, cos0_ref, sin0_ref), (q1_ref, cos1_ref, sin1_ref))
    for micro, (q_ref, cos_ref, sin_ref) in enumerate(tables):
        values = (x1_ref if micro else x_ref)[...].astype(jnp.float32)
        normed = (values * norm_scaling(values, 0) * gain_ref[:, 0:1]).astype(jnp.bfloat16)
        n_ref[:, micro * TOK : (micro + 1) * TOK] = normed
        linear = dot32(tall, normed)
        cosine, sine = cos_ref[...], sin_ref[...]
        for head in range(HEADS + KV_HEADS):
            low = head * HEAD_DIM
            former = linear[low : low + half_width]
            latter = linear[low + half_width : low + HEAD_DIM]
            turned = jnp.concatenate(
                [former * cosine - latter * sine, latter * cosine + former * sine], axis=0
            ).astype(jnp.bfloat16)
            if head < HEADS:
                scaled = turned.astype(jnp.float32) * 0.125
                q_ref[head // GROUPS, head % GROUPS] = scaled.astype(jnp.bfloat16)
            else:
                low = low - D
                kv_ref[micro, low : low + HEAD_DIM, :] = turned
        kv_ref[micro, KV_WIDTH:, :] = linear[D + KV_WIDTH :].astype(jnp.bfloat16)


def project(near, following, tokens, tokens_1, gain_columns, tables):
    low = jnp.bfloat16
    return pl.pallas_call(
        project_kernel,
        out_shape=(
            jax.ShapeDtypeStruct(heads_shape, low),
            jax.ShapeDtypeStruct(heads_shape, low),
            jax.ShapeDtypeStruct((2, 2 * KV_WIDTH, TOK), low),
            jax.ShapeDtypeStruct((D, D + 2 * KV_WIDTH), low),
            jax.ShapeDtypeStruct((D, D), low),
            jax.ShapeDtypeStruct((D, 2 * TOK), low),
        ),
        in_specs=[vmem()] * 9,
        out_specs=(vmem(),) * 6,
        scratch_shapes=[
            pltpu.VMEM((D * FF // 128, 128), jnp.float32),
            pltpu.VMEM((5, D, 128), jnp.float32),
        ],
        compiler_params=kernel_params,
        cost_estimate=pl.CostEstimate(
            flops=4 * TOK * D * 960, bytes_accessed=8000000, transcendentals=0
        ),
        name="project",
    )(near, following, tokens, tokens_1, gain_columns, *tables[0], *tables[1])


def projection_kernel(
    n_ref, dq0_ref, dq1_ref, kept0_ref, kept1_ref, got_ref, far_ref,
    cos0_ref, sin0_ref, cos1_ref, sin1_ref, gwo_ref, tie_ref,
    keep_ref, send_ref, all_ref, held, cut,
):
    spot = chunk_spot()
    half_width = HEAD_DIM // 2
    parts = ((dq0_ref, kept0_ref, cos0_ref, sin0_ref), (dq1_ref, kept1_ref, cos1_ref, sin1_ref))
    for micro, (dq_ref, kept_ref, cos_ref, sin_ref) in enumerate(parts):
        columns = slice(micro * TOK, (micro + 1) * TOK)
        all_ref[:D, columns] = dq_ref[...]
        cosine, sine = cos_ref[...], sin_ref[...]
        summed = kept_ref[0].astype(jnp.float32) + got_ref[micro].astype(jnp.float32)
        if micro == 0:
            summed = summed + far_ref[...].astype(jnp.float32)
        for head in range(KV_HEADS):
            low = head * HEAD_DIM
            former = summed[low : low + half_width, :]
            latter = summed[low + half_width : low + HEAD_DIM, :]
            all_ref[D + low : D + low + half_width, columns] = (
                former * cosine + latter * sine
            ).astype(jnp.bfloat16)
            all_ref[D + low + half_width : D + low + HEAD_DIM, columns] = (
                latter * cosine - former * sine
            ).astype(jnp.bfloat16)
        all_ref[D + KV_WIDTH :, columns] = summed[KV_WIDTH:, :].astype(jnp.bfloat16)
    held[:, : D + 2 * KV_WIDTH] = dot_with(n_ref[...], all_ref[...], 1, 1)
    held[:, D + 2 * KV_WIDTH :] = gwo_ref[...].astype(jnp.float32)
    for side in range(COL_CUT):
        start = (side ^ lax.rem(spot, COL_CUT)) * CHUNK_COLS
        cut[...] = held[:, pl.ds(pl.multiple_of(start, CHUNK_COLS), CHUNK_COLS)]
        for index, part in row_parts(cut, spot, side):
            (keep_ref, send_ref)[index // 4][index % 4] = part


def projection_grads(normed, dqs, kept, got, far, tables, gwo, tie):
    rows = normed.shape[1]
    chunk_shape = (CHUNKS // 2, CHUNK_ROWS, CHUNK_COLS)
    return pl.pallas_call(
        projection_kernel,
        out_shape=(
            jax.ShapeDtypeStruct(chunk_shape, jnp.bfloat16),
            jax.ShapeDtypeStruct(chunk_shape, jnp.bfloat16),
            jax.ShapeDtypeStruct((D + 2 * KV_WIDTH, rows), jnp.bfloat16),
        ),
        in_specs=[vmem()] * 12 + [anywhere()],
        out_specs=(vmem(),) * 3,
        scratch_shapes=[
            pltpu.VMEM((D, FF), jnp.float32),
            pltpu.VMEM((D, CHUNK_COLS), jnp.float32),
        ],
        compiler_params=kernel_params,
        cost_estimate=pl.CostEstimate(
            flops=2 * rows * D * 960, bytes_accessed=8000000, transcendentals=0
        ),
        name="projection_grads",
    )(normed, *dqs, *kept, got, far, *tables[0], *tables[1], gwo, tie)


def both(left_ref, right_ref, where=...):
    total = left_ref[where].astype(jnp.float32) + right_ref[where].astype(jnp.float32)
    return total.astype(jnp.bfloat16)


def plain_call(kernel, outs, operands, ties, name):
    outs = [jax.ShapeDtypeStruct(shape, jnp.bfloat16) for shape in outs]
    ties = ties if isinstance(ties, tuple) else (ties,)
    count = len(operands)

    def run(*refs):
        kernel(*refs[: count + 1], *refs[count + len(ties) :])

    return pl.pallas_call(
        run,
        out_shape=outs,
        in_specs=[vmem()] * count + [anywhere()] * len(ties),
        out_specs=[vmem()] * len(outs),
        compiler_params=kernel_params,
        name=name,
    )(*operands, *ties)


def turns_kernel(keep_ref, got_ref, early_ref, tie_ref, *outs):
    quarter = positions()[0]
    for shift, out in enumerate(outs):
        target = lax.rem(quarter + shift, 4)

        @pl.when(target == 0)
        def _():
            out[...] = both(keep_ref, got_ref, 0)

        @pl.when(target != 0)
        def _():
            out[...] = early_ref[jnp.maximum(target - 1, 0)]


def depth_turns(keep, got, early, tie):
    return plain_call(turns_kernel, [keep.shape[1:]] * 4, (keep, got, early), tie, "depth_turns")


def sum_kernel(*refs):
    total = refs[0][...].astype(jnp.float32)
    for ref in refs[1:-2]:
        total = total + ref[...].astype(jnp.float32)
    refs[-1][...] = total.astype(jnp.bfloat16)


def tied_sum(operands, tie):
    return plain_call(sum_kernel, [operands[0].shape], operands, tie, "tied_sum")[0]


def late_kernel(keep_ref, got_ref, tie_ref, keep_out, send_out):
    size = keep_out.shape[0]
    keep_out[...] = both(keep_ref, got_ref, slice(0, size))
    send_out[...] = both(keep_ref, got_ref, slice(size, 2 * size))


def late_halves(keep, got, tie):
    shape = (keep.shape[0] // 2, *keep.shape[1:])
    return plain_call(late_kernel, [shape] * 2, (keep, got), tie, "late_halves")


def pair_kernel(first_ref, second_ref, tie_ref, out_ref):
    out_ref[:1] = first_ref[...]
    out_ref[1:] = second_ref[...]


def tied_pair(first, second, tie):
    shape = (3, *first.shape[1:])
    return plain_call(pair_kernel, [shape], (first, second), tie, "tied_pair")[0]


def pick_first_kernel(own_ref, got1_ref, got2_ref, got3_ref, tie_ref, out_ref):
    quarter = positions()[0]
    for place, ref in enumerate((own_ref, got1_ref, got2_ref, got3_ref)):

        @pl.when(quarter == place)
        def _():
            out_ref[...] = ref[...]


def pick_first(pieces, tie):
    return plain_call(pick_first_kernel, [pieces[0].shape], pieces, tie, "pick_first")[0]


def pick_rest_kernel(own_ref, got1_ref, got2_ref, got3_ref, tie_ref, gu_ref, d_ref):
    quarter = positions()[0]

    def run(flat, tiles):
        for place, out in ((1, gu_ref), (2, gu_ref), (3, d_ref)):
            for shift, ref in enumerate((own_ref, got1_ref, got2_ref, got3_ref)):

                @pl.when(lax.rem(quarter - place + 4, 4) == shift)
                def _():
                    flat[...] = ref[...].astype(jnp.float32)

            rows, width = out.shape
            if width > D:
                for tile in range(FF // 128):
                    low = (place - 1) * FF + tile * 128
                    out[:, low : low + 128] = flat[
                        pl.ds(tile, rows, stride=FF // 128), :
                    ].astype(jnp.bfloat16)
            else:
                unflatten(flat, 0, rows, width, tiles)
                for tile, low, breadth in tile_widths(width):
                    out[:, low : low + breadth] = tiles[tile][:, :breadth].astype(jnp.bfloat16)

    pl.run_scoped(
        run,
        pltpu.VMEM(own_ref.shape, jnp.float32),
        pltpu.VMEM((5, FF // CHUNKS, 128), jnp.float32),
    )


def pick_rest(pieces, tie):
    shapes = [(D // CHUNKS, 2 * FF), (FF // CHUNKS, D)]
    return plain_call(pick_rest_kernel, shapes, pieces, tie, "pick_rest")


def cast_kernel(value_ref, tie_ref, out_ref):
    out_ref[...] = value_ref[...].astype(out_ref.dtype)


def tied_cast(value, tie):
    return pl.pallas_call(
        cast_kernel,
        out_shape=jax.ShapeDtypeStruct(value.shape, jnp.bfloat16),
        in_specs=[vmem(), anywhere()],
        out_specs=vmem(),
        compiler_params=kernel_params,
        name="tied_cast",
    )(value, tie)


def inputs_kernel(
    all_ref, w_ref, x_ref, x1_ref, dh_ref, gain_ref, tie_ref, out_ref, out1_ref, gg_ref
):
    gain = gain_ref[:, 0:1]
    total = jnp.zeros((D, 1), jnp.float32)
    for micro in range(2):
        columns = slice(micro * TOK, (micro + 1) * TOK)
        upstream = dot32(w_ref[...], all_ref[:, columns])
        values = (x1_ref if micro else x_ref)[...].astype(jnp.float32)
        part, gain_grad = norm_back(values, norm_scaling(values, 0), gain, upstream, 0)
        total = total + gain_grad
        grad = dh_ref[micro] + part
        store_result(micro, grad, out_ref, out1_ref)
    gg_ref[...] = jnp.broadcast_to(total, gg_ref.shape)


def input_grads(grad_qkv, w_qkv, tokens, tokens_1, grad_state, gain_columns, tie):
    return pl.pallas_call(
        inputs_kernel,
        out_shape=(
            jax.ShapeDtypeStruct((2, D, TOK), jnp.float32),
            jax.ShapeDtypeStruct((D, TOK), jnp.bfloat16),
            jax.ShapeDtypeStruct((D, 128), jnp.float32),
        ),
        in_specs=[vmem()] * 6 + [anywhere()],
        out_specs=(vmem(),) * 3,
        compiler_params=kernel_params,
        cost_estimate=pl.CostEstimate(
            flops=4 * TOK * D * 960, bytes_accessed=8000000, transcendentals=0
        ),
        name="input_grads",
    )(grad_qkv, w_qkv, tokens, tokens_1, grad_state, gain_columns, tie)


def place_kernel(whole_ref, part_ref, tie_ref, out_ref):
    out_ref[0] = part_ref[...].astype(out_ref.dtype)


def place_last(whole, part, tie):
    return pl.pallas_call(
        place_kernel,
        out_shape=jax.ShapeDtypeStruct(whole.shape, whole.dtype),
        grid=(1,),
        in_specs=[anywhere(), pl.BlockSpec(part.shape, lambda step: (0, 0)), anywhere()],
        out_specs=pl.BlockSpec((1, *part.shape), lambda step: (1, 0, 0)),
        input_output_aliases={0: 0},
        compiler_params=kernel_params,
        name="place_last",
    )(whole, part, tie)


def newton_loop(matrix, scale):
    current = matrix / (jnp.sqrt(jnp.sum(matrix * matrix)) + frobenius_epsilon)

    def iterate(unused, held):
        low = held.astype(jnp.bfloat16)
        square = dot_with(low, low, 1, 1)
        square_low = square.astype(jnp.bfloat16)
        mixer = newton_second * square + newton_third * dot32(square_low, square_low)
        return newton_first * held + dot32(mixer.astype(jnp.bfloat16), low)

    return lax.fori_loop(0, NS_STEPS, iterate, current) * (0.2 * math.sqrt(scale))


def newton_wide(total):
    def run(low, square, square_low, mixer, step):
        height, breadth = total.shape
        block = 256

        def scale_by(factor, keep_low):
            for row in range(0, height, 16):
                part = total[row : row + 16, :] * factor
                total[row : row + 16, :] = part
                if keep_low:
                    low[row : row + 16, :] = part.astype(jnp.bfloat16)

        norm = jnp.zeros((8, breadth), jnp.float32)
        for row in range(0, height, 8):
            part = total[row : row + 8, :]
            norm = norm + part * part
        scale_by(1.0 / (jnp.sqrt(jnp.sum(norm)) + frobenius_epsilon), True)

        def iterate(unused, held):
            square[...] = dot_with(low[...], low[...], 1, 1)
            for row in range(0, height, 16):
                rows = slice(row, row + 16)
                square_low[rows, :] = square[rows, :].astype(jnp.bfloat16)
            step[:, :height] = dot32(square_low[...], square_low[...])
            for row in range(0, height, 16):
                rows = slice(row, row + 16)
                mixed = newton_second * square[rows, :] + newton_third * step[rows, :height]
                mixer[rows, :] = mixed.astype(jnp.bfloat16)
            for column in range(0, breadth, block):
                columns = slice(column, column + block)
                step[:, :block] = dot32(mixer[...], low[:, columns])
                for row in range(0, height, 32):
                    rows = slice(row, row + 32)
                    part = newton_first * total[rows, columns] + step[rows, :block]
                    total[rows, columns] = part
                    low[rows, columns] = part.astype(jnp.bfloat16)
            return held

        lax.fori_loop(0, NS_STEPS, iterate, 0)
        scale_by(0.2 * math.sqrt(breadth), False)

    height, breadth = total.shape
    pl.run_scoped(
        run,
        pltpu.VMEM((height, breadth), jnp.bfloat16),
        pltpu.VMEM((height, height), jnp.float32),
        pltpu.VMEM((height, height), jnp.bfloat16),
        pltpu.VMEM((height, height), jnp.bfloat16),
        pltpu.VMEM((height, height), jnp.float32),
    )


def flatten_rows(tiles, start, rows, width, out):
    pairs, step, whole = rows // 2, width * 2 // 128, width // 128
    spans = range(whole + 1)
    even = [tiles[place, pl.ds(start, pairs, stride=2), :] for place in spans]
    odd = [tiles[place, pl.ds(start + 1, pairs, stride=2), :] for place in spans]
    for place in range(whole):
        out[pl.ds(place, pairs, stride=step), :] = even[place]
    rest = width - whole * 128
    joined = jnp.concatenate([even[whole][:, :rest]] + odd[:whole] + [odd[whole][:, :rest]], axis=1)
    for place in range(whole, step):
        low = (place - whole) * 128
        out[pl.ds(place, pairs, stride=step), :] = joined[:, low : low + 128]


def shard_rows(kind, kinds, start, matrix, tiles, out):
    length = out.shape[0] * 128

    if 0 in kinds:

        @pl.when(kind == 0)
        def _():
            rows = length // FF
            for place in range(FF // 128):
                out[pl.ds(place, rows, stride=FF // 128), :] = matrix[
                    pl.ds(pl.multiple_of(start, 8), rows), place * 128 : (place + 1) * 128
                ]

        @pl.when(kind == 5)
        def _():
            window = pl.multiple_of(lax.div(start, 128) * 128, 128)
            for place, low, breadth in tile_widths(D):
                part = matrix[low : low + breadth, pl.ds(window, 256)]
                tiles[place, :256, :breadth] = part.T
            flatten_rows(tiles, start - window, length // D, D, out)

    for place, (base, low, width) in zip((1, 3, 4, 2), MIXED):
        if place not in kinds:
            continue

        @pl.when(kind == place)
        def _():
            for tile, column, breadth in tile_widths(width):
                tiles[tile, :D, :breadth] = matrix[:, low + column : low + column + breadth]
            flatten_rows(tiles, start, length // width, width, out)


def own_kind(length):
    square, narrow = D * D, D * KV_WIDTH
    quarter = lax.axis_index("quarter")
    index = lax.axis_index("rep") * 2 + lax.axis_index("half")
    within = (index * lax.axis_size("ctx") + lax.axis_index("ctx")) * length
    kind = jnp.where(quarter == 3, 5, 0)
    start = jnp.where(quarter == 3, lax.div(within, D), lax.div(within, FF))
    edges = ((0, 1, D), (square, 3, KV_WIDTH), (square + narrow, 4, KV_WIDTH))
    for edge, place, width in (*edges, (square + 2 * narrow, 2, D)):
        inside = (quarter == 0) & (within >= edge)
        kind = jnp.where(inside, place, kind)
        start = jnp.where(inside, lax.div(within - edge, width), start)
    return (kind, start)


def load_matrix(kind, old_ref, flat, total, tiles):
    flat[...] = old_ref[...].astype(jnp.float32) * momentum_decay

    @pl.when(kind == 0)
    def _():
        for place in range(FF // 128):
            columns = slice(place * 128, (place + 1) * 128)
            total[:, columns] = flat[pl.ds(place, D, stride=FF // 128), :]

    @pl.when(kind == 5)
    def _():
        unflatten(flat, 0, FF, D, tiles)
        for place, low, breadth in tile_widths(D):
            total[low : low + breadth, :] = tiles[place].T[:breadth]

    for place, (base, low, width) in zip((1, 3, 4, 2), MIXED):

        @pl.when(kind == place)
        def _():
            unflatten(flat, base, D, width, tiles)
            for tile, column, breadth in tile_widths(width):
                total[:, low + column : low + column + breadth] = tiles[tile][:D, :breadth]


def update_matrix(kind, kinds, total):
    if 0 in kinds:

        @pl.when((kind == 0) | (kind == 5))
        def _():
            newton_wide(total)

    for place, (base, low, width) in zip((1, 3, 4, 2), MIXED):
        if place not in kinds:
            continue

        @pl.when(kind == place)
        def _():
            columns = slice(low, low + width)
            if width == D:
                total[:, columns] = newton_loop(total[:, columns], D)
            else:
                total[:, columns] = newton_loop(total[:, columns].T, D).T


def momentum_kernel(length, old_ref, tie_ref, out_ref, flat, tiles):
    kind = own_kind(length)[0]
    load_matrix(kind, old_ref, flat, out_ref, tiles)


def lay_momentum(length, old, tie):
    return pl.pallas_call(
        partial(momentum_kernel, length),
        out_shape=jax.ShapeDtypeStruct((D, FF), jnp.float32),
        in_specs=[vmem(), anywhere()],
        out_specs=vmem(),
        scratch_shapes=[
            pltpu.VMEM((D * FF // 128, 128), jnp.float32),
            pltpu.VMEM((5, FF, 128), jnp.float32),
        ],
        compiler_params=kernel_params,
        name="lay_momentum",
    )(old, tie)


def newton_kernel(local, length, *refs):
    count = 3 if local else 2
    grad, total, tiles = refs[-3:]
    outs = refs[-3 - count : -3]
    pieces, (old_ref, *rest) = refs[:2], refs[2:-3]
    kind, start = own_kind(length)
    spot = chunk_spot()

    def run():
        for index in range(CHUNKS):
            chunk = spot ^ index
            row = pl.multiple_of(lax.div(chunk, COL_CUT) * CHUNK_ROWS, CHUNK_ROWS)
            column = pl.multiple_of(lax.rem(chunk, COL_CUT) * CHUNK_COLS, CHUNK_COLS)
            rows, columns = pl.ds(row, CHUNK_ROWS), pl.ds(column, CHUNK_COLS)
            part = pieces[index // 4][index % 4]
            grad[rows, columns] = part.astype(jnp.float32)
            total[rows, columns] = old_ref[rows, columns] + part.astype(jnp.float32)
        kinds = (0, 1, 2, 3, 4, 5)
        update_matrix(kind, kinds, total)
        if local:
            weights_ref, momentum_ref = rest[:2]
            grad_ref, new_momentum_ref, new_weights_ref = outs
            shard_rows(kind, kinds, start, grad, tiles, grad_ref)
            shard_rows(kind, kinds, start, total, tiles, new_weights_ref)
            new_momentum_ref[...] = momentum_decay * momentum_ref[...] + grad_ref[...]
            new_weights_ref[...] = (
                weights_ref[...] * (1.0 - matrix_rate * weight_decay)
                - matrix_rate * new_weights_ref[...]
            )
        else:
            outs[0][...] = grad[...]
            outs[1][...] = total[...]

    run()


def newton(length, pieces, old, shards):
    local = len(shards) > 0
    if local:
        outs = (jax.ShapeDtypeStruct(shards[0].shape, jnp.float32),) * 3
    else:
        outs = (jax.ShapeDtypeStruct((D, FF), jnp.float32),) * 2
    operands = (*pieces, old, *shards)

    return pl.pallas_call(
        partial(newton_kernel, local, length),
        out_shape=outs,
        in_specs=[vmem()] * len(operands),
        out_specs=(vmem(),) * len(outs),
        scratch_shapes=[
            pltpu.VMEM((D, FF), jnp.float32),
            pltpu.VMEM((D, FF), jnp.float32),
            pltpu.VMEM((5, FF, 128), jnp.float32),
        ],
        compiler_params=kernel_params,
        cost_estimate=pl.CostEstimate(
            flops=12000000000, bytes_accessed=9000000, transcendentals=0
        ),
        name="newton",
    )(*operands)


def own_rows(kind, row, shard_length, gradient, update):
    def block_case(low, width):
        def run(gradient, update):
            start = (row, low)
            size = (shard_length // width, width)
            return tuple(
                lax.dynamic_slice(whole, start, size).reshape(-1) for whole in (gradient, update)
            )

        return run

    def tall_case(gradient, update):
        start = (0, row)
        size = (D, shard_length // D)
        return tuple(
            lax.dynamic_slice(whole, start, size).T.reshape(-1) for whole in (gradient, update)
        )

    cases = [
        block_case(0, FF),
        block_case(0, D),
        block_case(FF - D, D),
        block_case(D, KV_WIDTH),
        block_case(D + KV_WIDTH, KV_WIDTH),
        tall_case,
    ]
    return lax.switch(kind, cases, gradient, update)


CORE_SWAP = [(0, 1), (1, 0), (2, 3), (3, 2)]
CHIP_SWAP = [(0, 2), (2, 0), (1, 3), (3, 1)]
SIDE_SWAP = [(0, 1), (1, 0)]
END_SWAP = [(0, 3), (3, 0), (1, 2), (2, 1)]


def plane_swap(value, bit):
    axis, swap = (("ctx", CHIP_SWAP), ("half", SIDE_SWAP), ("ctx", CORE_SWAP))[bit]
    return lax.ppermute(value, axis, swap)


def low_sum(left, right):
    return (left.astype(jnp.float32) + right.astype(jnp.float32)).astype(jnp.bfloat16)


def low_total(first, others):
    total = first.astype(jnp.float32)
    for part in others:
        total = total + part.astype(jnp.float32)
    return total.astype(jnp.bfloat16)


def plane_gather(piece, swap):
    pieces = piece[None]
    for bit in range(2):
        pieces = jnp.concatenate([pieces, swap(pieces, bit)], axis=0)
    return (pieces, swap(pieces, 2))


def depth_shift(value, shift, targets):
    pairs = [(place, (place + shift) % 4) for place in range(4)]
    return lax.ppermute(value, "quarter", [pair for pair in pairs if pair[1] in targets])


def gather_weights(low, tie):
    if lax.axis_size("rep") > 1:
        full = lax.all_gather(low, EVERY, axis=0, tiled=True).reshape(4, D * FF)
        ctx = lax.axis_index("ctx")
        spot = lax.rem(ctx, 2) * 4 + lax.axis_index("half") * 2 + ctx // 2
        chunk = jnp.arange(CHUNKS, dtype=jnp.int32) ^ spot
        order = 4 * (chunk // 2 % 2) + 2 * (chunk % 2) + chunk // 4
        mixed = full[0].reshape(CHUNKS, -1, 128)[order]
        return (mixed[:4], mixed[4:]), [
            jnp.concatenate([full[1].reshape(D, FF), full[2].reshape(D, FF)], axis=1),
            full[3].reshape(FF, D),
        ]
    first = [lax.ppermute(low, "quarter", [(0, shift)]) for shift in range(1, 4)]
    mixed = pick_first((low, *first), tie)
    others = [
        lax.ppermute(low, "quarter", [(place, (place + shift) % 4) for place in range(1, 4)])
        for shift in range(1, 4)
    ]
    rest = [
        lax.all_gather(piece, PLANE, axis=0, tiled=True)
        for piece in pick_rest((low, *others), mixed)
    ]
    return plane_gather(mixed, plane_swap), rest


def per_device(tokens, lengths, weights, momentum, norm_gains, gain_first, gain_second, cotangent):
    ctx = lax.axis_index("ctx")
    chip = ctx // 2
    reps = lax.axis_size("rep")
    shard_length = weights.shape[0]
    flat_shape = (shard_length // 128, 128)
    lengths = lengths[:, 0]
    tokens = jnp.swapaxes(tokens, 1, 2)
    cotangent = jnp.swapaxes(cotangent, 1, 2)
    gain_columns = norm_gains.T

    tokens_1 = lax.ppermute(tokens[1], "ctx", END_SWAP)
    mixed_weights, (w_gate_up, w_down) = gather_weights(
        weights.reshape(flat_shape).astype(jnp.bfloat16), tokens_1
    )
    near = chip == 0

    def slots(first, second):
        return jnp.where(near, first, second), jnp.where(near, second, first)

    x0, x1 = slots(tokens[0], tokens_1)
    begin_rows, tables = [], []
    for micro, own_lengths in enumerate(slots(lengths[0], lengths[1])):
        own_places = own_block(micro) * TOK + jnp.arange(TOK, dtype=jnp.int32)
        offsets, begins = layout(own_lengths, own_places)
        begin_rows.append(begins.reshape(1, TOK))
        tables.append(rope_tables(offsets))

    q0, q1, keyvals, w_qkv, w_out, normed = project(
        *mixed_weights, x0, x1, gain_columns, tables
    )
    queries = (q0, q1)
    far = lax.ppermute(keyvals[0], "ctx", CHIP_SWAP)
    keyvals = (
        keyvals,
        lax.ppermute(keyvals, "ctx", CORE_SWAP),
        far,
        lax.ppermute(far, "ctx", CORE_SWAP),
    )
    mixed, log_totals = [], []
    for micro in range(2):
        mixed_one, log_total = attend_forward(
            micro, lengths, queries[micro], keyvals, begin_rows[micro], norm_gains
        )
        mixed.append(mixed_one)
        log_totals.append(log_total)
    cotangent_1 = lax.ppermute(tied_cast(cotangent[1], mixed[0]), "ctx", END_SWAP)
    old = lax.all_gather(
        tied_cast(momentum.reshape(flat_shape), mixed[0]),
        ("rep", "half", "ctx"),
        axis=0,
        tiled=True,
    )
    outs = mlp(
        x0,
        x1,
        cotangent,
        cotangent_1,
        [part.reshape(D, TOK) for part in mixed],
        w_out,
        w_gate_up,
        w_down,
        norm_gains[1:2],
    )
    result, result_1, grad_state, grad_mixed_0, grad_mixed_1 = outs[:5]
    keep, send, grad_w_out, gain_two_grad = outs[5:]
    returned = lax.ppermute(result_1, "ctx", END_SWAP)

    def back_pass(micro, grad_mixed, tie):
        return attend_back(
            micro,
            lengths,
            queries[micro],
            keyvals,
            begin_rows[micro],
            mixed[micro],
            log_totals[micro],
            grad_mixed.reshape(heads_shape),
            *tables[micro],
            tie,
        )

    got = plane_swap(send, 2)
    dq0, kept0, sent0 = back_pass(0, grad_mixed_0, norm_gains)
    keep, send = late_halves(keep, got, dq0)
    got = plane_swap(send, 1)
    dq1, kept1, sent1 = back_pass(1, grad_mixed_1, keep)
    keep, send = late_halves(keep, got, (dq1, old, returned))
    traded = lax.ppermute(tied_pair(sent0, sent1, keep), "ctx", CORE_SWAP)
    crossed = lax.ppermute(low_sum(kept1[1], traded[2]), "ctx", CHIP_SWAP)
    got = plane_swap(send, 0)
    late_keep, late_send, grad_qkv = projection_grads(
        normed,
        (dq0.reshape(D, TOK), dq1.reshape(D, TOK)),
        (kept0, kept1),
        traded,
        crossed,
        tables,
        grad_w_out,
        keep,
    )
    late_got = plane_swap(late_send, 2)
    late_keep, late_send = late_halves(late_keep, late_got, norm_gains)
    late_got = plane_swap(late_send, 1)
    grad_inputs, grad_inputs_1, gain_one_grad = input_grads(
        grad_qkv, w_qkv, x0, x1, grad_state, gain_columns, late_keep
    )
    early = tied_sum((keep[0], got[0]), gain_one_grad)
    late_keep, late_send = late_halves(late_keep, late_got, early)
    gain_grad = jnp.concatenate([gain_one_grad[:, 0].reshape(1, D), gain_two_grad], axis=0)
    gain_grad = gain_grad + sum(
        lax.ppermute(gain_grad, "ctx", [(place, place ^ turn) for place in range(4)])
        for turn in range(1, 4)
    )
    piece, *turns = depth_turns(late_keep, plane_swap(late_send, 0), early, gain_grad)
    parts = [depth_shift(turn, shift, range(4)) for shift, turn in enumerate(turns, start=1)]
    gain_grad = gain_grad + sum(depth_shift(gain_grad, shift, range(4)) for shift in range(1, 4))
    old = lay_momentum(shard_length, old, piece)
    piece = tied_sum((piece, *parts), (old, gain_grad))
    if reps > 1:
        piece = lax.psum(piece, "rep")
        gain_grad = lax.psum(gain_grad, "rep")
    pieces = plane_gather(piece, plane_swap)
    gain_grad = gain_grad + plane_swap(gain_grad, 1)
    grad_inputs_1 = lax.ppermute(grad_inputs_1, "ctx", END_SWAP)

    shards = ()
    if flat_shape[0] % 8 == 0:
        shards = (weights.reshape(flat_shape), momentum.reshape(flat_shape))
    outs = newton(shard_length, pieces, old, shards)
    if len(shards) > 0:
        grad_shard, new_momentum, new_weights = [out.reshape(weights.shape) for out in outs]
    else:
        kind, start = own_kind(shard_length)
        grad_shard, update_shard = own_rows(kind, start, shard_length, *outs)
        new_momentum = momentum_decay * momentum + grad_shard
        new_weights = weights * (1.0 - matrix_rate * weight_decay) - matrix_rate * update_shard

    def placed(whole, part):
        whole = lax.dynamic_update_index_in_dim(whole, part.astype(jnp.float32), 1, 0)
        return jnp.swapaxes(whole, 1, 2)

    first_new = first_decay * gain_first + (1.0 - first_decay) * gain_grad
    second_new = second_decay * gain_second + (1.0 - second_decay) * gain_grad * gain_grad
    debiased_first_moment = first_new / (1.0 - first_decay**ADAM_STEP)
    corrected_second = second_new / (1.0 - second_decay**ADAM_STEP)
    new_gains = norm_gains * (
        1.0 - gain_rate * weight_decay
    ) - gain_rate * debiased_first_moment / (jnp.sqrt(corrected_second) + adam_epsilon)
    return (
        placed(result, returned),
        jnp.swapaxes(place_last(grad_inputs, grad_inputs_1, outs[-1]), 1, 2),
        grad_shard,
        new_momentum,
        new_weights,
        first_new,
        second_new,
        new_gains,
    )


def solution(mesh):
    devices = mesh.devices
    count = devices.size
    context = mesh.shape["ctx"]
    split = Mesh(
        devices.reshape(4, count // (8 * context), 2, context), ("quarter", "rep", "half", "ctx")
    )
    rows = P(None, EVERY, None)
    flat = P(EVERY)
    placed = (rows, P(None, ("quarter", "rep", "half"), None), flat, flat, P(), P(), P(), rows)
    return jax.shard_map(
        per_device,
        mesh=split,
        in_specs=placed,
        out_specs=(rows, rows, flat, flat, flat, P(), P(), P()),
        check_vma=False,
    )
```

profile of v0, /device:TPU:8, one launch (start us, length us, event | category | flops | bytes accessed | tf_op | source)
XLA Modules:
  0.0 378.6 jit_solution(16267720526846437091)
XLA Ops:
  7.2 1.1 slice_bitcast_fusion.1
  8.3 1.0 collective-permute-start
  9.3 1.0 bitcast_convert_fusion.refs_0_
  10.4 1.4 collective-permute-start.1
  13.2 3.5 collective-permute-start.11
  16.7 4.0 %collective-permute-done.1.refs_1_ = bf16[864,128]{1,0:T(8,128)(2,1)S(1)} collective-permute-done((bf16[864,128]{1,0:T(8,128)(2,1)S(1)}, bf16[864,128]{1,0:T(8,128)(2,1)S(1)}, u32[]{:S(2)}, u32[]{:S(2)}) %collective-permute-start.1) | collective-permute-done | bytes 221216 | tf_op jit(solution)/shard_map/ppermute | solution.py:1210
  20.7 3.4 collective-permute-start.12
  24.1 2.8 collective-permute-start.13
  28.5 2.0 pick_first.1.refs_4_
  30.5 1.5 collective-permute-done.11.refs_1_
  32.0 4.4 %collective-permute-done.12.refs_2_ = bf16[864,128]{1,0:T(8,128)(2,1)S(1)} collective-permute-done((bf16[864,128]{1,0:T(8,128)(2,1)S(1)}, bf16[864,128]{1,0:T(8,128)(2,1)S(1)}, u32[]{:S(2)}, u32[]{:S(2)}) %collective-permute-start.12) | collective-permute-done | bytes 221216 | tf_op jit(solution)/shard_map/ppermute | solution.py:1213
  36.4 5.7 %collective-permute-done.13.refs_3_ = bf16[864,128]{1,0:T(8,128)(2,1)S(1)} collective-permute-done((bf16[864,128]{1,0:T(8,128)(2,1)S(1)}, bf16[864,128]{1,0:T(8,128)(2,1)S(1)}, u32[]{:S(2)}, u32[]{:S(2)}) %collective-permute-start.13) | collective-permute-done | bytes 221216 | tf_op jit(solution)/shard_map/ppermute | solution.py:1213
  42.8 2.4 pick_rest.1
  46.9 6.5 %collective-permute-done.4 = bf16[1,864,128]{2,1,0:T(8,128)(2,1)S(1)} collective-permute-done((bf16[1,864,128]{2,1,0:T(8,128)(2,1)S(1)}, bf16[1,864,128]{2,1,0:T(8,128)(2,1)S(1)}, u32[]{:S(2)}, u32[]{:S(2)}) %collective-permute-start.4) | collective-permute-done | bytes 221216 | tf_op jit(solution)/shard_map/ppermute | solution.py:1172
  53.5 1.6 collective-permute-start.5
  55.1 10.5 %collective-permute-done.5 = bf16[2,864,128]{2,1,0:T(8,128)(2,1)S(1)} collective-permute-done((bf16[2,864,128]{2,1,0:T(8,128)(2,1)S(1)}, bf16[2,864,128]{2,1,0:T(8,128)(2,1)S(1)}, u32[]{:S(2)}, u32[]{:S(2)}) %collective-permute-start.5) | collective-permute-done | bytes 442400 | tf_op jit(solution)/shard_map/ppermute | solution.py:1172
  66.8 1.2 multiply_sine_fusion
  68.0 1.1 broadcast_select_fusion
  69.2 7.8 %project.1 = (bf16[3,3,64,512]{3,2,1,0:T(8,128)(2,1)}, bf16[3,3,64,512]{3,2,1,0:T(8,128)(2,1)}, bf16[2,384,512]{2,1,0:T(8,128)(2,1)}, bf16[576,960]{1,0:T(8,128)...) custom-call(bf16[4,864,128]{2,1,0:T(8,128)(2,1)} %copy-done.11, ...), custom_call_target="tpu_custom_call" | custom-call | flops 1132462080 | bytes 8000000 | tf_op jit(solution)/shard_map/project/pallas_call | solution.py:613
  76.9 1.0 slice_bitcast_fusion.3
  78.0 1.5 collective-permute-start.8
  79.7 13.2 %collective-permute-done.8.far_ref = bf16[384,512]{1,0:T(8,128)(2,1)S(1)} collective-permute-done((bf16[384,512]{1,0:T(8,128)(2,1)S(1)}, bf16[384,512]{1,0:T(8,128)(2,1)S(1)}, u32[]{:S(2)}, u32[]{:S(2)}) %collective-permute-start.8) | collective-permute-done | bytes 393248 | tf_op jit(solution)/shard_map/ppermute | solution.py:1255
  95.7 8.7 %attend_forward.2 = (bf16[3,3,64,512]{3,2,1,0:T(8,128)(2,1)}, f32[3,3,1,512]{3,2,1,0:T(1,128)}) custom-call(s32[2,4]{1,0:T(2,128)} %bitcast.79, bf16[3,3,64,512]{3,2,1,0:T(8,128)(2,1)} %get-tuple-element.56.q_ref, bf16[2,384,512]{2,1,0:T(8,128)(2,1)} %get-tuple-element.57.kv_ref, bf16[2,384,512]{2,1,0:T(8,128)(2,1)} %copy-done.43, ...), custom_call_target="tpu_custom_call" | custom-call | flops 2415919104 | bytes 4000000 | tf_op jit(solution)/shard_map/attend_forward/pallas_call | solution.py:335
  104.4 1.9 tied_cast.2
  106.3 2.1 collective-permute-start.10
  109.1 25.6 %attend_forward.3 = (bf16[3,3,64,512]{3,2,1,0:T(8,128)(2,1)}, f32[3,3,1,512]{3,2,1,0:T(1,128)}) custom-call(s32[2,4]{1,0:T(2,128)} %bitcast.80, bf16[3,3,64,512]{3,2,1,0:T(8,128)(2,1)} %get-tuple-element.59.q_ref, bf16[2,384,512]{2,1,0:T(8,128)(2,1)} %get-tuple-element.57.kv_ref, bf16[2,384,512]{2,1,0:T(8,128)(2,1)} %copy-done.43, ...), custom_call_target="tpu_custom_call" | custom-call | flops 2415919104 | bytes 4000000 | tf_op jit(solution)/shard_map/attend_forward/pallas_call | solution.py:335
  135.5 39.0 %mlp.1 = (f32[2,576,512]{2,1,0:T(8,128)}, bf16[576,512]{1,0:T(8,128)(2,1)}, f32[2,576,512]{2,1,0:T(8,128)}, bf16[576,512]{1,0:T(8,128)(2,1)}, bf16[576,512]{1,0:...) custom-call(bf16[576,512]{1,0:T(8,128)(2,1)} %get-tuple-element.108., ...), custom_call_target="tpu_custom_call" | custom-call | flops 16307453952 | bytes 25000000 | tf_op jit(solution)/shard_map/mlp/pallas_call | solution.py:504
  174.4 1.7 tied_cast.3
  176.2 10.6 %attend_back.2 = (bf16[3,3,64,512]{3,2,1,0:T(8,128)(2,1)}, bf16[1,384,512]{2,1,0:T(8,128)(2,1)}, bf16[1,384,512]{2,1,0:T(8,128)(2,1)}) custom-call(s32[2,4]{1,0:T(2,128)} %bitcast.81, bf16[3,3,64,512]{3,2,1,0:T(8,128)(2,1)} %get-tuple-element.56.q_ref, bf16[2,384,512]{2,1,0:T(8,128)(2,1)} %get-tuple-element.57.kv_ref, bf16[2,384,512]{2,1,0:T(8,128)(2,1)} %copy-done.43, ...), custom_call_target="tpu_custom_call" | custom-call | flops 6039797760 | bytes 8000000 | tf_op jit(solution)/shard_map/attend_back/pallas_call | solution.py:361
  186.8 1.5 copy-done.1
  188.2 4.5 %late_halves.4 = (bf16[2,3,144,768]{3,2,1,0:T(8,128)(2,1)}, bf16[2,3,144,768]{3,2,1,0:T(8,128)(2,1)}) custom-call(bf16[4,3,144,768]{3,2,1,0:T(8,128)(2,1)} %get-tuple-element.72.refs_0_, bf16[4,3,144,768]{3,2,1,0:T(8,128)(2,1)} %copy-done.1, bf16[3,3,64,512]{3,2,1,0:T(8,128)(2,1)} %get-tuple-element.69.refs_2_), custom_call_target="tpu_custom_call" | custom-call | tf_op jit(solution)/shard_map/late_halves/pallas_call | solution.py:709
  192.8 35.2 %attend_back.3 = (bf16[3,3,64,512]{3,2,1,0:T(8,128)(2,1)}, bf16[2,384,512]{2,1,0:T(8,128)(2,1)}, bf16[2,384,512]{2,1,0:T(8,128)(2,1)}) custom-call(s32[2,4]{1,0:T(2,128)} %bitcast.82, bf16[3,3,64,512]{3,2,1,0:T(8,128)(2,1)} %get-tuple-element.59.q_ref, bf16[2,384,512]{2,1,0:T(8,128)(2,1)} %get-tuple-element.57.kv_ref, bf16[2,384,512]{2,1,0:T(8,128)(2,1)} %copy-done.43, ...), custom_call_target="tpu_custom_call" | custom-call | flops 6039797760 | bytes 8000000 | tf_op jit(solution)/shard_map/attend_back/pallas_call | solution.py:361
  229.2 2.9 late_halves.5
  232.2 2.4 tied_pair.1
  234.6 3.1 collective-permute-done.17.got_ref
  237.7 1.8 collective-permute-start.18
  239.6 9.6 %collective-permute-done.18.far_ref = bf16[384,512]{1,0:T(8,128)(2,1)S(1)} collective-permute-done((bf16[384,512]{1,0:T(8,128)(2,1)S(1)}, bf16[384,512]{1,0:T(8,128)(2,1)S(1)}, u32[]{:S(2)}, u32[]{:S(2)}) %collective-permute-start.18) | collective-permute-done | bytes 393248 | tf_op jit(solution)/shard_map/ppermute | solution.py:1312
  250.0 7.0 %projection_grads.1 = (bf16[4,144,768]{2,1,0:T(8,128)(2,1)}, bf16[4,144,768]{2,1,0:T(8,128)(2,1)}, bf16[960,1024]{1,0:T(8,128)(2,1)}) custom-call(bf16[576,1024]{1,0:T(8,128)(2,1)} %get-tuple-element.66.n_ref, bf16[576,512]{1,0:T(8,128)(2,1)} %bitcast.57, bf16[576,512]{1,0:T(8,128)(2,1)} %bitcast.58, bf16[1,384,512]{2,1,0:T(8,128)(2,1)} %get-tuple-element.76.kept0_ref, ...), custom_call_target="tpu_custom_call" | custom-call | flops 1132462080 | bytes 8000000 | tf_op jit(solution)/shard_map/projection_grads/pallas_call | solution.py:675
  256.9 1.8 collective-permute-start.22
  260.5 2.4 late_halves.6
  262.9 2.0 collective-permute-start.21
  264.9 7.6 %input_grads.1 = (f32[2,576,512]{2,1,0:T(8,128)}, bf16[576,512]{1,0:T(8,128)(2,1)}, f32[576,128]{1,0:T(8,128)}) custom-call(bf16[960,1024]{1,0:T(8,128)(2,1)} %get-tuple-element.83.all_ref, bf16[576,960]{1,0:T(8,128)(2,1)} %get-tuple-element.84.w_ref, bf16[576,512]{1,0:T(8,128)(2,1)} %get-tuple-element.108.x_ref, ...), custom_call_target="tpu_custom_call" | custom-call | flops 1132462080 | bytes 8000000 | tf_op jit(solution)/shard_map/input_grads/pallas_call | solution.py:849
  272.6 1.1 slice_reduce_fusion
  273.8 1.8 collective-permute-start.25
  276.6 2.3 tied_sum.2.refs_2_
  279.6 2.0 late_halves.7
  281.6 1.7 collective-permute-start.23
  283.5 1.9 collective-permute-start.32
  285.5 4.0 %collective-permute-done.23.refs_1_ = bf16[1,144,768]{2,1,0:T(8,128)(2,1)S(1)} collective-permute-done((bf16[1,144,768]{2,1,0:T(8,128)(2,1)}, bf16[1,144,768]{2,1,0:T(8,128)(2,1)S(1)}, u32[]{:S(2)}, u32[]{:S(2)}) %collective-permute-start.23) | collective-permute-done | bytes 221216 | tf_op jit(solution)/shard_map/ppermute | solution.py:1172
  290.2 2.4 depth_turns.1
  293.3 1.3 collective-permute-start.29
  294.6 1.3 add_add_fusion.refs_5_
  295.9 3.8 %lay_momentum.1.refs_4_.refs_2_ = f32[576,1536]{1,0:T(8,128)} custom-call(bf16[6912,128]{1,0:T(8,128)(2,1)} %all-gather.8.cloned.1.call-done.refs_3_.old_ref, bf16[144,768]{1,0:T(8,128)(2,1)} %get-tuple-element.97.tie_ref.refs_0_), custom_call_target="tpu_custom_call" | custom-call | tf_op jit(solution)/shard_map/lay_momentum/pallas_call | solution.py:1059
  299.7 1.4 collective-permute-done.27.refs_1_
  301.1 10.6 %collective-permute-done.28.refs_2_ = bf16[144,768]{1,0:T(8,128)(2,1)S(1)} collective-permute-done((bf16[144,768]{1,0:T(8,128)(2,1)}, bf16[144,768]{1,0:T(8,128)(2,1)S(1)}, u32[]{:S(2)}, u32[]{:S(2)}) %collective-permute-start.28) | collective-permute-done | bytes 221216 | tf_op jit(solution)/shard_map/ppermute | solution.py:1195
  313.3 2.2 tied_sum.3
  315.5 1.6 collective-permute-start.33
  317.1 6.0 %collective-permute-done.33 = bf16[1,144,768]{2,1,0:T(8,128)(2,1)S(1)} collective-permute-done((bf16[1,144,768]{2,1,0:T(8,128)(2,1)}, bf16[1,144,768]{2,1,0:T(8,128)(2,1)S(1)}, u32[]{:S(2)}, u32[]{:S(2)}) %collective-permute-start.33) | collective-permute-done | bytes 221216 | tf_op jit(solution)/shard_map/ppermute | solution.py:1172
  323.1 1.0 pad_maximum_fusion.3
  324.4 11.0 %collective-permute-done.34 = bf16[2,144,768]{2,1,0:T(8,128)(2,1)S(1)} collective-permute-done((bf16[2,144,768]{2,1,0:T(8,128)(2,1)S(1)}, bf16[2,144,768]{2,1,0:T(8,128)(2,1)S(1)}, u32[]{:S(2)}, u32[]{:S(2)}) %collective-permute-start.34) | collective-permute-done | bytes 442400 | tf_op jit(solution)/shard_map/ppermute | solution.py:1172
  335.4 1.0 pad_maximum_fusion.1.refs_0_
  337.1 3.1 collective-permute-done.36
  341.8 27.1 %newton.1 = (f32[864,128]{1,0:T(8,128)}, f32[864,128]{1,0:T(8,128)}, f32[864,128]{1,0:T(8,128)}) custom-call(bf16[4,144,768]{2,1,0:T(8,128)(2,1)} %copy-done.12, bf16[4,144,768]{2,1,0:T(8,128)(2,1)} %copy-done.42, f32[576,1536]{1,0:T(8,128)} %lay_momentum.1.refs_4_.refs_2_, f32[864,128]{1,0:T(8,128)} %bitcast.72, f32[864,128]{1,0:T(8,128)} %bitcast.71), custom_call_target="tpu_custom_call" | custom-call | flops 12000000000 | bytes 9000000 | tf_op jit(solution)/shard_map/newton/pallas_call | solution.py:1117
  369.7 2.2 place_last.1
  (172 shorter events, 23.2 us)
Async XLA Ops:
  7.2 127.5 %all-gather.6.cloned.1.call-start = ((), (), s32[]{:S(2)}) async-start(), calls=%async_computation.1 | async-start | bytes 2211840 | tf_op jit(solution)/shard_map/all_gather | solution.py:1217
  8.3 18.7 %collective-permute-start = (bf16[576,512]{1,0:T(8,128)(2,1)S(1)}, bf16[576,512]{1,0:T(8,128)(2,1)S(1)}, u32[]{:S(2)}, u32[]{:S(2)}) collective-permute-start(bf16[576,512]{1,0:T(8,128)(2,1)S(1)} %slice_bitcast_fusion.1), channel_id=1, source_target_pairs={{0,3},{3,0},{1,2},{2,1},{4,7},{7,4},{5,6},{6,5},{8,11},{11,8},{9,1... | collective-permute-start | bytes 1769480 | tf_op jit(solution)/shard_map/ppermute | solution.py:1234
  10.4 16.6 %copy-start.7 = (bf16[864,128]{1,0:T(8,128)(2,1)}, bf16[864,128]{1,0:T(8,128)(2,1)S(1)}, u32[]{:S(2)}) copy-start(bf16[864,128]{1,0:T(8,128)(2,1)S(1)} %bitcast_convert_fusion.refs_0_) | copy-start | bytes 663556
  10.4 36.2 %copy-start.39 = (s32[2,1,4]{2,1,0:T(1,128)S(1)}, s32[2,1,4]{2,1,0:T(1,128)}, u32[]{:S(2)}) copy-start(s32[2,1,4]{2,1,0:T(1,128)} %param.9) | copy-start | bytes 100
  10.4 10.3 %collective-permute-start.1 = (bf16[864,128]{1,0:T(8,128)(2,1)S(1)}, bf16[864,128]{1,0:T(8,128)(2,1)S(1)}, u32[]{:S(2)}, u32[]{:S(2)}) collective-permute-start(bf16[864,128]{1,0:T(8,128)(2,1)S(1)} %bitcast_convert_fusion.refs_0_), channel_id=1, source_target_pairs={{0,8},{1,9},{2,10},{3,11},{4,12},{5,13},{6,14},{7,15}} | collective-permute-start | bytes 663560 | tf_op jit(solution)/shard_map/ppermute | solution.py:1210
  11.8 12.3 %collective-permute-start.2 = (bf16[864,128]{1,0:T(8,128)(2,1)S(1)}, bf16[864,128]{1,0:T(8,128)(2,1)S(1)}, u32[]{:S(2)}, u32[]{:S(2)}) collective-permute-start(bf16[864,128]{1,0:T(8,128)(2,1)S(1)} %bitcast_convert_fusion.refs_0_), channel_id=1, source_target_pairs={{0,16},{1,17},{2,18},{3,19},{4,20},{5,21},{6,22},{7,23}} | collective-permute-start | bytes 663560 | tf_op jit(solution)/shard_map/ppermute | solution.py:1210
  12.5 14.5 %collective-permute-start.3 = (bf16[864,128]{1,0:T(8,128)(2,1)S(1)}, bf16[864,128]{1,0:T(8,128)(2,1)S(1)}, u32[]{:S(2)}, u32[]{:S(2)}) collective-permute-start(bf16[864,128]{1,0:T(8,128)(2,1)S(1)} %bitcast_convert_fusion.refs_0_), channel_id=1, source_target_pairs={{0,24},{1,25},{2,26},{3,27},{4,28},{5,29},{6,30},{7,31}} | collective-permute-start | bytes 663560 | tf_op jit(solution)/shard_map/ppermute | solution.py:1210
  13.2 18.8 %collective-permute-start.11 = (bf16[864,128]{1,0:T(8,128)(2,1)S(1)}, bf16[864,128]{1,0:T(8,128)(2,1)S(1)}, u32[]{:S(2)}, u32[]{:S(2)}) collective-permute-start(bf16[864,128]{1,0:T(8,128)(2,1)S(1)} %bitcast_convert_fusion.refs_0_), channel_id=1, source_target_pairs={{8,16},{16,24},{24,0},{9,17},{17,25},{25,1},{10,18},{18,26},{26,2}... | collective-permute-start | bytes 663560 | tf_op jit(solution)/shard_map/ppermute | solution.py:1213
  20.7 6.3 %copy-start.20 = (bf16[864,128]{1,0:T(8,128)(2,1)}, bf16[864,128]{1,0:T(8,128)(2,1)S(1)}, u32[]{:S(2)}) copy-start(bf16[864,128]{1,0:T(8,128)(2,1)S(1)} %collective-permute-done.1.refs_1_) | copy-start | bytes 663556
  20.7 15.7 %collective-permute-start.12 = (bf16[864,128]{1,0:T(8,128)(2,1)S(1)}, bf16[864,128]{1,0:T(8,128)(2,1)S(1)}, u32[]{:S(2)}, u32[]{:S(2)}) collective-permute-start(bf16[864,128]{1,0:T(8,128)(2,1)S(1)} %bitcast_convert_fusion.refs_0_), channel_id=1, source_target_pairs={{8,24},{16,0},{24,8},{9,25},{17,1},{25,9},{10,26},{18,2},{26,10},{... | collective-permute-start | bytes 663560 | tf_op jit(solution)/shard_map/ppermute | solution.py:1213
  24.1 18.0 %collective-permute-start.13 = (bf16[864,128]{1,0:T(8,128)(2,1)S(1)}, bf16[864,128]{1,0:T(8,128)(2,1)S(1)}, u32[]{:S(2)}, u32[]{:S(2)}) collective-permute-start(bf16[864,128]{1,0:T(8,128)(2,1)S(1)} %bitcast_convert_fusion.refs_0_), channel_id=1, source_target_pairs={{8,0},{16,8},{24,16},{9,1},{17,9},{25,17},{10,2},{18,10},{26,18},{... | collective-permute-start | bytes 663560 | tf_op jit(solution)/shard_map/ppermute | solution.py:1213
  30.5 15.5 %copy-start = (bf16[864,128]{1,0:T(8,128)(2,1)S(1)}, bf16[864,128]{1,0:T(8,128)(2,1)}, u32[]{:S(2)}) copy-start(bf16[864,128]{1,0:T(8,128)(2,1)} %pick_first.1.refs_4_) | copy-start | bytes 663556
  32.0 10.1 %copy-start.24 = (bf16[864,128]{1,0:T(8,128)(2,1)}, bf16[864,128]{1,0:T(8,128)(2,1)S(1)}, u32[]{:S(2)}) copy-start(bf16[864,128]{1,0:T(8,128)(2,1)S(1)} %collective-permute-done.11.refs_1_) | copy-start | bytes 663556
  45.1 20.7 %copy-start.29 = (f32[2,576]{1,0:T(2,128)S(1)}, f32[2,576]{1,0:T(2,128)}, u32[]{:S(2)}) copy-start(f32[2,576]{1,0:T(2,128)} %refs_2_.1) | copy-start | bytes 13828
  45.2 89.5 %all-gather.4.cloned.1.call-start = ((), (), s32[]{:S(2)}) async-start(), calls=%async_computation | async-start | bytes 3981312 | tf_op jit(solution)/shard_map/all_gather | solution.py:1217
  45.2 22.8 %copy-start.3 = (bf16[576,512]{1,0:T(8,128)(2,1)S(1)}, bf16[576,512]{1,0:T(8,128)(2,1)}, u32[]{:S(2)}) copy-start(bf16[576,512]{1,0:T(8,128)(2,1)} %copy-done.2) | copy-start | bytes 1769476
  45.2 22.8 %copy-start.10 = (bf16[2,512,576]{1,2,0:T(8,128)(2,1)S(1)}, bf16[2,512,576]{1,2,0:T(8,128)(2,1)}, u32[]{:S(2)}) copy-start(bf16[2,512,576]{1,2,0:T(8,128)(2,1)} %param.8) | copy-start | bytes 3538948
  45.9 182.0 %all-gather.8.cloned.1.call-start = ((), (), s32[]{:S(2)}) async-start(), calls=%async_computation.2 | async-start | bytes 1990656 | tf_op jit(solution)/shard_map/all_gather | solution.py:1270
  46.0 7.4 %collective-permute-start.4 = (bf16[1,864,128]{2,1,0:T(8,128)(2,1)S(1)}, bf16[1,864,128]{2,1,0:T(8,128)(2,1)S(1)}, u32[]{:S(2)}, u32[]{:S(2)}) collective-permute-start(bf16[1,864,128]{2,1,0:T(8,128)(2,1)S(1)} %bitcast.54), channel_id=1, source_target_pairs={{0,2},{2,0},{1,3},{3,1},{4,6},{6,4},{5,7},{7,5},{8,10},{10,8},{9,1... | collective-permute-start | bytes 663560 | tf_op jit(solution)/shard_map/ppermute | solution.py:1172
  53.5 12.2 %collective-permute-start.5 = (bf16[2,864,128]{2,1,0:T(8,128)(2,1)S(1)}, bf16[2,864,128]{2,1,0:T(8,128)(2,1)S(1)}, u32[]{:S(2)}, u32[]{:S(2)}) collective-permute-start(bf16[2,864,128]{2,1,0:T(8,128)(2,1)S(1)} %pad_maximum_fusion.2), channel_id=1, source_target_pairs={{0,4},{4,0},{1,5},{5,1},{2,6},{6,2},{3,7},{7,3},{8,12},{12,8},{9,1... | collective-permute-start | bytes 1327112 | tf_op jit(solution)/shard_map/ppermute | solution.py:1172
  55.1 14.0 %copy-start.35 = (s32[512]{0:T(512)}, s32[512]{0:T(512)S(1)}, u32[]{:S(2)}) copy-start(s32[512]{0:T(512)S(1)} %get-tuple-element.119) | copy-start | bytes 6148
  55.1 14.0 %copy-start.36 = (s32[512]{0:T(512)}, s32[512]{0:T(512)S(1)}, u32[]{:S(2)}) copy-start(s32[512]{0:T(512)S(1)} %get-tuple-element.120) | copy-start | bytes 6148
  65.8 3.4 collective-permute-start.6
  69.2 23.8 %copy-start.18 = (bf16[2,512,576]{1,2,0:T(8,128)(2,1)S(1)}, bf16[2,512,576]{1,2,0:T(8,128)(2,1)}, u32[]{:S(2)}) copy-start(bf16[2,512,576]{1,2,0:T(8,128)(2,1)} %param.15) | copy-start | bytes 3538948
  78.0 15.0 %collective-permute-start.8 = (bf16[384,512]{1,0:T(8,128)(2,1)S(1)}, bf16[384,512]{1,0:T(8,128)(2,1)S(1)}, u32[]{:S(2)}, u32[]{:S(2)}) collective-permute-start(bf16[384,512]{1,0:T(8,128)(2,1)S(1)} %slice_bitcast_fusion.3), channel_id=1, source_target_pairs={{0,2},{2,0},{1,3},{3,1},{4,6},{6,4},{5,7},{7,5},{8,10},{10,8},{9,1... | collective-permute-start | bytes 1179656 | tf_op jit(solution)/shard_map/ppermute | solution.py:1255
  79.5 15.2 %collective-permute-start.7 = (bf16[2,384,512]{2,1,0:T(8,128)(2,1)}, bf16[2,384,512]{2,1,0:T(8,128)(2,1)S(1)}, u32[]{:S(2)}, u32[]{:S(2)}) collective-permute-start(bf16[2,384,512]{2,1,0:T(8,128)(2,1)} %get-tuple-element.57.kv_ref), channel_id=1, source_target_pairs={{0,1},{1,0},{2,3},{3,2},{4,5},{5,4},{6,7},{7,6},{8,9},{9,8},{10,11... | collective-permute-start | bytes 2359304 | tf_op jit(solution)/shard_map/ppermute | solution.py:1258
  92.9 1.7 collective-permute-start.9
  106.3 28.3 %collective-permute-start.10 = (bf16[576,512]{1,0:T(8,128)(2,1)}, bf16[576,512]{1,0:T(8,128)(2,1)S(1)}, u32[]{:S(2)}, u32[]{:S(2)}) collective-permute-start(bf16[576,512]{1,0:T(8,128)(2,1)} %tied_cast.2), channel_id=1, source_target_pairs={{0,3},{3,0},{1,2},{2,1},{4,7},{7,4},{5,6},{6,5},{8,11},{11,8},{9,1... | collective-permute-start | bytes 1769480 | tf_op jit(solution)/shard_map/ppermute | solution.py:1269
  174.4 12.3 %collective-permute-start.15 = (bf16[4,3,144,768]{3,2,1,0:T(8,128)(2,1)}, bf16[4,3,144,768]{3,2,1,0:T(8,128)(2,1)S(1)}, u32[]{:S(2)}, u32[]{:S(2)}) collective-permute-start(bf16[4,3,144,768]{3,2,1,0:T(8,128)(2,1)} %get-tuple-element.73), channel_id=1, source_target_pairs={{0,1},{1,0},{2,3},{3,2},{4,5},{5,4},{6,7},{7,6},{8,9},{9,8},{10,11... | collective-permute-start | bytes 7962632 | tf_op jit(solution)/shard_map/ppermute | solution.py:1172
  192.7 35.2 %collective-permute-start.16 = (bf16[2,3,144,768]{3,2,1,0:T(8,128)(2,1)}, bf16[2,3,144,768]{3,2,1,0:T(8,128)(2,1)S(1)}, u32[]{:S(2)}, u32[]{:S(2)}) collective-permute-start(bf16[2,3,144,768]{3,2,1,0:T(8,128)(2,1)} %get-tuple-element.80), channel_id=1, source_target_pairs={{0,4},{4,0},{1,5},{5,1},{2,6},{6,2},{3,7},{7,3},{8,12},{12,8},{9,1... | collective-permute-start | bytes 3981320 | tf_op jit(solution)/shard_map/ppermute | solution.py:1172
  192.8 35.2 %collective-permute-start.14 = (bf16[576,512]{1,0:T(8,128)(2,1)S(1)}, bf16[576,512]{1,0:T(8,128)(2,1)S(1)}, u32[]{:S(2)}, u32[]{:S(2)}) collective-permute-start(bf16[576,512]{1,0:T(8,128)(2,1)S(1)} %copy-done.46), channel_id=1, source_target_pairs={{0,3},{3,0},{1,2},{2,1},{4,7},{7,4},{5,6},{6,5},{8,11},{11,8},{9,1... | collective-permute-start | bytes 1769480 | tf_op jit(solution)/shard_map/ppermute | solution.py:1289
  234.6 3.1 collective-permute-start.17
  237.6 11.6 %copy-start.6 = (bf16[3,384,512]{2,1,0:T(8,128)(2,1)}, bf16[3,384,512]{2,1,0:T(8,128)(2,1)S(1)}, u32[]{:S(2)}) copy-start(bf16[3,384,512]{2,1,0:T(8,128)(2,1)S(1)} %collective-permute-done.17.got_ref) | copy-start | bytes 3538948
  237.7 11.5 %collective-permute-start.18 = (bf16[384,512]{1,0:T(8,128)(2,1)S(1)}, bf16[384,512]{1,0:T(8,128)(2,1)S(1)}, u32[]{:S(2)}, u32[]{:S(2)}) collective-permute-start(bf16[384,512]{1,0:T(8,128)(2,1)S(1)} %fusion), channel_id=1, source_target_pairs={{0,2},{2,0},{1,3},{3,1},{4,6},{6,4},{5,7},{7,5},{8,10},{10,8},{9,1... | collective-permute-start | bytes 1179656 | tf_op jit(solution)/shard_map/ppermute | solution.py:1312
  250.0 7.0 %copy-start.44 = (bf16[1,3,144,768]{3,2,1,0:T(8,128)(2,1)S(1)}, bf16[1,3,144,768]{3,2,1,0:T(8,128)(2,1)}, u32[]{:S(2)}) copy-start(bf16[1,3,144,768]{3,2,1,0:T(8,128)(2,1)} %get-tuple-element.92) | copy-start | bytes 1990660
  256.9 2.6 collective-permute-start.19
  256.9 18.8 %collective-permute-start.22 = (bf16[1,3,144,768]{3,2,1,0:T(8,128)(2,1)S(1)}, bf16[1,3,144,768]{3,2,1,0:T(8,128)(2,1)S(1)}, u32[]{:S(2)}, u32[]{:S(2)}) collective-permute-start(bf16[1,3,144,768]{3,2,1,0:T(8,128)(2,1)S(1)} %copy-done.44), channel_id=1, source_target_pairs={{0,2},{2,0},{1,3},{3,1},{4,6},{6,4},{5,7},{7,5},{8,10},{10,8},{9,1... | collective-permute-start | bytes 1990664 | tf_op jit(solution)/shard_map/ppermute | solution.py:1172
  262.9 16.0 %collective-permute-start.21 = (bf16[2,144,768]{2,1,0:T(8,128)(2,1)}, bf16[2,144,768]{2,1,0:T(8,128)(2,1)S(1)}, u32[]{:S(2)}, u32[]{:S(2)}) collective-permute-start(bf16[2,144,768]{2,1,0:T(8,128)(2,1)} %get-tuple-element.91), channel_id=1, source_target_pairs={{0,4},{4,0},{1,5},{5,1},{2,6},{6,2},{3,7},{7,3},{8,12},{12,8},{9,1... | collective-permute-start | bytes 1327112 | tf_op jit(solution)/shard_map/ppermute | solution.py:1172
  264.9 8.8 %copy-start.34 = (f32[1,576]{1,0:T(1,128)S(1)}, f32[1,576]{1,0:T(1,128)}, u32[]{:S(2)}) copy-start(f32[1,576]{1,0:T(1,128)} %get-tuple-element.96) | copy-start | bytes 6916
  273.8 9.6 %collective-permute-start.24 = (f32[2,576]{1,0:T(2,128)S(1)}, f32[2,576]{1,0:T(2,128)S(1)}, u32[]{:S(2)}, u32[]{:S(2)}) collective-permute-start(f32[2,576]{1,0:T(2,128)S(1)} %pad_maximum_fusion.4), channel_id=1, source_target_pairs={{0,1},{1,0},{2,3},{3,2},{4,5},{5,4},{6,7},{7,6},{8,9},{9,8},{10,11... | collective-permute-start | bytes 13832 | tf_op jit(solution)/shard_map/ppermute | solution.py:1334
  273.8 9.5 %collective-permute-start.25 = (f32[2,576]{1,0:T(2,128)S(1)}, f32[2,576]{1,0:T(2,128)S(1)}, u32[]{:S(2)}, u32[]{:S(2)}) collective-permute-start(f32[2,576]{1,0:T(2,128)S(1)} %pad_maximum_fusion.4), channel_id=1, source_target_pairs={{0,2},{1,3},{2,0},{3,1},{4,6},{5,7},{6,4},{7,5},{8,10},{9,11},{10,... | collective-permute-start | bytes 13832 | tf_op jit(solution)/shard_map/ppermute | solution.py:1334
  275.6 7.7 %collective-permute-start.26 = (f32[2,576]{1,0:T(2,128)S(1)}, f32[2,576]{1,0:T(2,128)S(1)}, u32[]{:S(2)}, u32[]{:S(2)}) collective-permute-start(f32[2,576]{1,0:T(2,128)S(1)} %pad_maximum_fusion.4), channel_id=1, source_target_pairs={{0,3},{1,2},{2,1},{3,0},{4,7},{5,6},{6,5},{7,4},{8,11},{9,10},{10,... | collective-permute-start | bytes 13832 | tf_op jit(solution)/shard_map/ppermute | solution.py:1334
  281.6 7.9 %collective-permute-start.23 = (bf16[1,144,768]{2,1,0:T(8,128)(2,1)}, bf16[1,144,768]{2,1,0:T(8,128)(2,1)S(1)}, u32[]{:S(2)}, u32[]{:S(2)}) collective-permute-start(bf16[1,144,768]{2,1,0:T(8,128)(2,1)} %get-tuple-element.95), channel_id=1, source_target_pairs={{0,2},{2,0},{1,3},{3,1},{4,6},{6,4},{5,7},{7,5},{8,10},{10,8},{9,1... | collective-permute-start | bytes 663560 | tf_op jit(solution)/shard_map/ppermute | solution.py:1172
  283.4 6.1 %copy-start.33 = (f32[2,576]{1,0:T(2,128)}, f32[2,576]{1,0:T(2,128)S(1)}, u32[]{:S(2)}) copy-start(f32[2,576]{1,0:T(2,128)S(1)} %add_add_fusion.1.refs_3_) | copy-start | bytes 13828
  283.4 10.0 %collective-permute-start.30 = (f32[2,576]{1,0:T(2,128)S(1)}, f32[2,576]{1,0:T(2,128)S(1)}, u32[]{:S(2)}, u32[]{:S(2)}) collective-permute-start(f32[2,576]{1,0:T(2,128)S(1)} %add_add_fusion.1.refs_3_), channel_id=1, source_target_pairs={{0,8},{8,16},{16,24},{24,0},{1,9},{9,17},{17,25},{25,1},{2,10},{10... | collective-permute-start | bytes 13832 | tf_op jit(solution)/shard_map/ppermute | solution.py:1195
  283.4 11.1 %collective-permute-start.31 = (f32[2,576]{1,0:T(2,128)S(1)}, f32[2,576]{1,0:T(2,128)S(1)}, u32[]{:S(2)}, u32[]{:S(2)}) collective-permute-start(f32[2,576]{1,0:T(2,128)S(1)} %add_add_fusion.1.refs_3_), channel_id=1, source_target_pairs={{0,16},{8,24},{16,0},{24,8},{1,17},{9,25},{17,1},{25,9},{2,18},{10... | collective-permute-start | bytes 13832 | tf_op jit(solution)/shard_map/ppermute | solution.py:1195
  283.5 11.1 %collective-permute-start.32 = (f32[2,576]{1,0:T(2,128)S(1)}, f32[2,576]{1,0:T(2,128)S(1)}, u32[]{:S(2)}, u32[]{:S(2)}) collective-permute-start(f32[2,576]{1,0:T(2,128)S(1)} %add_add_fusion.1.refs_3_), channel_id=1, source_target_pairs={{0,24},{8,0},{16,8},{24,16},{1,25},{9,1},{17,9},{25,17},{2,26},{10... | collective-permute-start | bytes 13832 | tf_op jit(solution)/shard_map/ppermute | solution.py:1195
  292.5 8.6 %collective-permute-start.27 = (bf16[144,768]{1,0:T(8,128)(2,1)}, bf16[144,768]{1,0:T(8,128)(2,1)S(1)}, u32[]{:S(2)}, u32[]{:S(2)}) collective-permute-start(bf16[144,768]{1,0:T(8,128)(2,1)} %get-tuple-element.98), channel_id=1, source_target_pairs={{0,8},{8,16},{16,24},{24,0},{1,9},{9,17},{17,25},{25,1},{2,10},{10... | collective-permute-start | bytes 663560 | tf_op jit(solution)/shard_map/ppermute | solution.py:1195
  292.7 19.1 %collective-permute-start.28 = (bf16[144,768]{1,0:T(8,128)(2,1)}, bf16[144,768]{1,0:T(8,128)(2,1)S(1)}, u32[]{:S(2)}, u32[]{:S(2)}) collective-permute-start(bf16[144,768]{1,0:T(8,128)(2,1)} %get-tuple-element.99), channel_id=1, source_target_pairs={{0,16},{8,24},{16,0},{24,8},{1,17},{9,25},{17,1},{25,9},{2,18},{10... | collective-permute-start | bytes 663560 | tf_op jit(solution)/shard_map/ppermute | solution.py:1195
  293.3 19.3 %collective-permute-start.29 = (bf16[144,768]{1,0:T(8,128)(2,1)}, bf16[144,768]{1,0:T(8,128)(2,1)S(1)}, u32[]{:S(2)}, u32[]{:S(2)}) collective-permute-start(bf16[144,768]{1,0:T(8,128)(2,1)} %get-tuple-element.100), channel_id=1, source_target_pairs={{0,24},{8,0},{16,8},{24,16},{1,25},{9,1},{17,9},{25,17},{2,26},{10... | collective-permute-start | bytes 663560 | tf_op jit(solution)/shard_map/ppermute | solution.py:1195
  301.1 11.5 %copy-start.23 = (bf16[144,768]{1,0:T(8,128)(2,1)}, bf16[144,768]{1,0:T(8,128)(2,1)S(1)}, u32[]{:S(2)}) copy-start(bf16[144,768]{1,0:T(8,128)(2,1)S(1)} %collective-permute-done.27.refs_1_) | copy-start | bytes 663556
  313.3 23.6 %copy-start.40 = (f32[2,576,512]{2,1,0:T(8,128)S(1)}, f32[2,576,512]{2,1,0:T(8,128)}, u32[]{:S(2)}) copy-start(f32[2,576,512]{2,1,0:T(8,128)} %get-tuple-element.64) | copy-start | bytes 7077892
  315.5 21.0 %copy-start.32 = (f32[2,576]{1,0:T(2,128)S(1)}, f32[2,576]{1,0:T(2,128)}, u32[]{:S(2)}) copy-start(f32[2,576]{1,0:T(2,128)} %add_add_fusion.refs_5_) | copy-start | bytes 13828
  315.5 21.4 %copy-start.5 = (bf16[576,512]{1,0:T(8,128)(2,1)S(1)}, bf16[576,512]{1,0:T(8,128)(2,1)}, u32[]{:S(2)}) copy-start(bf16[576,512]{1,0:T(8,128)(2,1)} %copy-done.4) | copy-start | bytes 1769476
  315.5 7.6 %collective-permute-start.33 = (bf16[1,144,768]{2,1,0:T(8,128)(2,1)}, bf16[1,144,768]{2,1,0:T(8,128)(2,1)S(1)}, u32[]{:S(2)}, u32[]{:S(2)}) collective-permute-start(bf16[1,144,768]{2,1,0:T(8,128)(2,1)} %bitcast.61), channel_id=1, source_target_pairs={{0,2},{2,0},{1,3},{3,1},{4,6},{6,4},{5,7},{7,5},{8,10},{10,8},{9,1... | collective-permute-start | bytes 663560 | tf_op jit(solution)/shard_map/ppermute | solution.py:1172
  324.1 13.0 %copy-start.45 = (bf16[576,512]{1,0:T(8,128)(2,1)S(1)}, bf16[576,512]{1,0:T(8,128)(2,1)}, u32[]{:S(2)}) copy-start(bf16[576,512]{1,0:T(8,128)(2,1)} %get-tuple-element.90) | copy-start | bytes 1769476
  324.1 16.2 %copy-start.31 = (f32[2,576]{1,0:T(2,128)S(1)}, f32[2,576]{1,0:T(2,128)}, u32[]{:S(2)}) copy-start(f32[2,576]{1,0:T(2,128)} %refs_2_.1) | copy-start | bytes 13828
  324.1 16.1 %copy-start.37 = (f32[2,576]{1,0:T(2,128)S(1)}, f32[2,576]{1,0:T(2,128)}, u32[]{:S(2)}) copy-start(f32[2,576]{1,0:T(2,128)} %param.14) | copy-start | bytes 13828
  324.1 16.1 %copy-start.38 = (f32[2,576]{1,0:T(2,128)S(1)}, f32[2,576]{1,0:T(2,128)}, u32[]{:S(2)}) copy-start(f32[2,576]{1,0:T(2,128)} %param.13) | copy-start | bytes 13828
  324.1 11.3 %collective-permute-start.34 = (bf16[2,144,768]{2,1,0:T(8,128)(2,1)S(1)}, bf16[2,144,768]{2,1,0:T(8,128)(2,1)S(1)}, u32[]{:S(2)}, u32[]{:S(2)}) collective-permute-start(bf16[2,144,768]{2,1,0:T(8,128)(2,1)S(1)} %pad_maximum_fusion.3), channel_id=1, source_target_pairs={{0,4},{4,0},{1,5},{5,1},{2,6},{6,2},{3,7},{7,3},{8,12},{12,8},{9,1... | collective-permute-start | bytes 1327112 | tf_op jit(solution)/shard_map/ppermute | solution.py:1172
  336.4 4.4 %collective-permute-start.35 = (bf16[4,144,768]{2,1,0:T(8,128)(2,1)S(1)}, bf16[4,144,768]{2,1,0:T(8,128)(2,1)S(1)}, u32[]{:S(2)}, u32[]{:S(2)}) collective-permute-start(bf16[4,144,768]{2,1,0:T(8,128)(2,1)S(1)} %pad_maximum_fusion.1.refs_0_), channel_id=1, source_target_pairs={{0,1},{1,0},{2,3},{3,2},{4,5},{5,4},{6,7},{7,6},{8,9},{9,8},{10,11... | collective-permute-start | bytes 2654216 | tf_op jit(solution)/shard_map/ppermute | solution.py:1172
  336.5 3.7 collective-permute-start.36
  337.0 31.9 %copy-start.41 = (f32[2,576,512]{2,1,0:T(8,128)}, f32[2,576,512]{2,1,0:T(8,128)S(1)}, u32[]{:S(2)}) copy-start(f32[2,576,512]{2,1,0:T(8,128)S(1)} %convert_dynamic-update-slice_fusion) | copy-start | bytes 7077892
  337.1 31.8 %collective-permute-start.20 = (bf16[576,512]{1,0:T(8,128)(2,1)S(1)}, bf16[576,512]{1,0:T(8,128)(2,1)S(1)}, u32[]{:S(2)}, u32[]{:S(2)}) collective-permute-start(bf16[576,512]{1,0:T(8,128)(2,1)S(1)} %copy-done.45), channel_id=1, source_target_pairs={{0,3},{3,0},{1,2},{2,1},{4,7},{7,4},{5,6},{6,5},{8,11},{11,8},{9,1... | collective-permute-start | bytes 1769480 | tf_op jit(solution)/shard_map/ppermute | solution.py:1347
  (26 other events, 47.8 us)
Sparse Core Ops, SparseCore 0:
  45.3 28.1 all-gather.5
  76.0 36.1 all-gather.3
  176.3 25.5 all-gather.7
where the time goes:
time: 386 us; the launch traced here: 379 us
  Pallas kernels  204 us (53%)
  waiting for transfers between devices  97.9 us (25%)
  starting transfers between devices  35.5 us (9%)
  local copies, waits for them, and re-layouts  18.9 us (5%)
  between operations  14.5 us (4%)
  other arithmetic  8.17 us (2%)
    pallas_call x2, Pallas kernels, attend_back(): pl.pallas_call(partial(backward_kernel, micro), out_shape=(jax.ShapeDtype...  45.8 us
    ppermute x13, waiting for transfers between devices, plane_swap(): return lax.ppermute(value, axis, swap)  41.9 us
    pallas_call x1, Pallas kernels, mlp(): pl.pallas_call(mlp_kernel, out_shape=(jax.ShapeDtypeStruct((2, D, TOK), j...  39 us
    pallas_call x2, Pallas kernels, attend_forward(): pl.pallas_call(partial(forward_kernel, micro), out_shape=(jax.ShapeDtypeS...  34.3 us
    pallas_call x1, Pallas kernels, newton(): pl.pallas_call(partial(newton_kernel, local, length), out_shape=outs, in_...  27.1 us
    pallas_call x10, Pallas kernels, plain_call(): pl.pallas_call(run, out_shape=outs, in_specs=[vmem()] * count + [anywhere...  25.5 us
    unnamed x101, local copies, waits for them, and re-layouts  14.1 us
    ppermute x1, waiting for transfers between devices, per_device(): far = lax.ppermute(keyvals[0], 'ctx', CHIP_SWAP)  13.2 us
  transfers between devices with their start and end apart: 40, of which 18 were waited for; matrix products, arithmetic and copies ran while one was open for 3% of the time, Pallas kernels for 38%

commit v1 on v0

--- a/solution.py
+++ b/solution.py
@@ -229,9 +229,14 @@
 
 def backward_kernel(
     micro, lengths_ref, q_ref, kv_ref, other_ref, far_ref, far_other_ref, begin_ref, o_ref, lse_ref,
-    do_ref, cos_ref, sin_ref, tie_ref,
-    dq_ref, keep_ref, send_ref, k_nat, v_nat, k_tall, dk_ref, dv_ref, s_ref, g_ref, p_ref, ds_ref,
+    do_ref, cos_ref, sin_ref, *refs,
 ):
+    if micro:
+        first_ref, *refs = refs
+    tie_ref, dq_ref, keep_ref, send_ref, k_nat, v_nat, k_tall, dk_ref, dv_ref, *refs = refs
+    s_ref, g_ref, p_ref, ds_ref = refs
+    if micro:
+        send_ref[:1] = first_ref[...]
     own = own_block(micro)
     slots = key_slots(own, micro, kv_ref, other_ref, far_ref, far_other_ref)
     for block, source in slots:
@@ -296,23 +301,24 @@
     lax.fori_loop(0, KV_HEADS, one_group, 0)
     for place, (block, _) in enumerate(slots):
         out_ref = (keep_ref, send_ref)[place % 2]
+        index = place // 2 + micro * (place % 2)
 
         @pl.when(block <= own)
         def _():
             rows = block_rows(block)
             for group in range(KV_HEADS):
                 low = HEAD_DIM * group
-                out_ref[place // 2, low : low + HEAD_DIM, :] = dk_ref[group, rows, :].T.astype(
+                out_ref[index, low : low + HEAD_DIM, :] = dk_ref[group, rows, :].T.astype(
                     jnp.bfloat16
                 )
                 low = low + KV_WIDTH
-                out_ref[place // 2, low : low + HEAD_DIM, :] = dv_ref[group, rows, :].T.astype(
+                out_ref[index, low : low + HEAD_DIM, :] = dv_ref[group, rows, :].T.astype(
                     jnp.bfloat16
                 )
 
         @pl.when(block > own)
         def _():
-            out_ref[place // 2] = jnp.zeros((2 * KV_WIDTH, TOK), jnp.bfloat16)
+            out_ref[index] = jnp.zeros((2 * KV_WIDTH, TOK), jnp.bfloat16)
 
 
 def vmem():
@@ -355,17 +361,18 @@
 
 
 def attend_back(
-    micro, lengths, queries, keyvals, begins, mixed, log_total, grad_mixed, cosine, sine, tie
+    micro, lengths, queries, keyvals, begins, mixed, log_total, grad_mixed, cosine, sine, before, tie
 ):
     half_shape = (1 + micro, 2 * KV_WIDTH, TOK)
+    send_shape = (1 + 2 * micro, 2 * KV_WIDTH, TOK)
     return pl.pallas_call(
         partial(backward_kernel, micro),
         out_shape=(
             jax.ShapeDtypeStruct(heads_shape, jnp.bfloat16),
             jax.ShapeDtypeStruct(half_shape, jnp.bfloat16),
-            jax.ShapeDtypeStruct(half_shape, jnp.bfloat16),
+            jax.ShapeDtypeStruct(send_shape, jnp.bfloat16),
         ),
-        in_specs=[smem()] + [vmem()] * 11 + [anywhere()],
+        in_specs=[smem()] + [vmem()] * (11 + len(before)) + [anywhere()],
         out_specs=(vmem(),) * 3,
         scratch_shapes=[
             pltpu.VMEM((KV_HEADS, 4 * TOK, HEAD_DIM), jnp.bfloat16),
@@ -383,7 +390,7 @@
             flops=10 * 9 * 64 * TOK * 2048, bytes_accessed=8000000, transcendentals=9 * TOK * 2048
         ),
         name="attend_back",
-    )(lengths, queries, *keyvals, begins, mixed, log_total, grad_mixed, cosine, sine, tie)
+    )(lengths, queries, *keyvals, begins, mixed, log_total, grad_mixed, cosine, sine, *before, tie)
 
 
 def dot_with(left, right, left_side, right_side):
@@ -756,14 +763,39 @@
     return plain_call(late_kernel, [shape] * 2, (keep, got), tie, "late_halves")
 
 
-def pair_kernel(first_ref, second_ref, tie_ref, out_ref):
-    out_ref[:1] = first_ref[...]
-    out_ref[1:] = second_ref[...]
-
-
-def tied_pair(first, second, tie):
-    shape = (3, *first.shape[1:])
-    return plain_call(pair_kernel, [shape], (first, second), tie, "tied_pair")[0]
+def early_halves(keep, got, ties, passed=None):
+    count, quarters, rows, columns = keep.shape
+    held = () if passed is None else (passed,)
+
+    def block(size):
+        return pl.BlockSpec((size, 1, rows, columns), lambda place: (0, place, 0, 0))
+
+    def kernel(keep_ref, got_ref, *refs):
+        keep_out, send_out = refs[len(held) + len(ties) :][:2]
+        late_kernel(keep_ref, got_ref, None, keep_out, send_out)
+
+    half = jax.ShapeDtypeStruct((count // 2, quarters, rows, columns), jnp.bfloat16)
+    return pl.pallas_call(
+        kernel,
+        out_shape=[half, half] + [jax.ShapeDtypeStruct(one.shape, one.dtype) for one in held],
+        grid=(quarters,),
+        in_specs=[block(count)] * 2 + [anywhere()] * (len(held) + len(ties)),
+        out_specs=[block(count // 2)] * 2 + [anywhere()] * len(held),
+        input_output_aliases={2: 2} if held else {},
+        compiler_params=kernel_params,
+        name="early_halves",
+    )(keep, got, *held, *ties)
+
+
+def finish_kernel(keep_ref, got_ref, late_ref, late_got_ref, tie_ref, early_out, keep_out, send_out):
+    early_out[...] = both(keep_ref, got_ref, 0)
+    late_kernel(late_ref, late_got_ref, None, keep_out, send_out)
+
+
+def finish_early(keep, got, late_keep, late_got, tie):
+    half = (late_keep.shape[0] // 2, *late_keep.shape[1:])
+    operands = (keep, got, late_keep, late_got)
+    return plain_call(finish_kernel, [keep.shape[1:], half, half], operands, tie, "finish_early")
 
 
 def pick_first_kernel(own_ref, got1_ref, got2_ref, got3_ref, tie_ref, out_ref):
@@ -814,19 +846,14 @@
     return plain_call(pick_rest_kernel, shapes, pieces, tie, "pick_rest")
 
 
-def cast_kernel(value_ref, tie_ref, out_ref):
-    out_ref[...] = value_ref[...].astype(out_ref.dtype)
-
-
-def tied_cast(value, tie):
-    return pl.pallas_call(
-        cast_kernel,
-        out_shape=jax.ShapeDtypeStruct(value.shape, jnp.bfloat16),
-        in_specs=[vmem(), anywhere()],
-        out_specs=vmem(),
-        compiler_params=kernel_params,
-        name="tied_cast",
-    )(value, tie)
+def copies_kernel(first_ref, second_ref, tie_ref, first_out, second_out):
+    first_out[...] = first_ref[...].astype(jnp.bfloat16)
+    second_out[...] = second_ref[...]
+
+
+def low_copies(first, second, tie):
+    shapes = [first.shape, second.shape]
+    return plain_call(copies_kernel, shapes, (first, second), tie, "low_copies")
 
 
 def inputs_kernel(
@@ -1259,16 +1286,17 @@
         far,
         lax.ppermute(far, "ctx", CORE_SWAP),
     )
+    low_momentum, moving = low_copies(momentum.reshape(flat_shape), cotangent[1], q1)
     mixed, log_totals = [], []
     for micro in range(2):
         mixed_one, log_total = attend_forward(
-            micro, lengths, queries[micro], keyvals, begin_rows[micro], norm_gains
+            micro, lengths, queries[micro], keyvals, begin_rows[micro], (low_momentum, norm_gains)[micro]
         )
         mixed.append(mixed_one)
         log_totals.append(log_total)
-    cotangent_1 = lax.ppermute(tied_cast(cotangent[1], mixed[0]), "ctx", END_SWAP)
+    cotangent_1 = lax.ppermute(moving, "ctx", END_SWAP)
     old = lax.all_gather(
-        tied_cast(momentum.reshape(flat_shape), mixed[0]),
+        low_momentum,
         ("rep", "half", "ctx"),
         axis=0,
         tiled=True,
@@ -1288,7 +1316,7 @@
     keep, send, grad_w_out, gain_two_grad = outs[5:]
     returned = lax.ppermute(result_1, "ctx", END_SWAP)
 
-    def back_pass(micro, grad_mixed, tie):
+    def back_pass(micro, grad_mixed, before, tie):
         return attend_back(
             micro,
             lengths,
@@ -1299,16 +1327,17 @@
             log_totals[micro],
             grad_mixed.reshape(heads_shape),
             *tables[micro],
+            before,
             tie,
         )
 
     got = plane_swap(send, 2)
-    dq0, kept0, sent0 = back_pass(0, grad_mixed_0, norm_gains)
-    keep, send = late_halves(keep, got, dq0)
+    dq0, kept0, sent0 = back_pass(0, grad_mixed_0, (), norm_gains)
+    keep, send = early_halves(keep, got, (dq0,))
     got = plane_swap(send, 1)
-    dq1, kept1, sent1 = back_pass(1, grad_mixed_1, keep)
-    keep, send = late_halves(keep, got, (dq1, old, returned))
-    traded = lax.ppermute(tied_pair(sent0, sent1, keep), "ctx", CORE_SWAP)
+    dq1, kept1, sent = back_pass(1, grad_mixed_1, (sent0,), keep)
+    keep, send, sent = early_halves(keep, got, (old, returned), sent)
+    traded = lax.ppermute(sent, "ctx", CORE_SWAP)
     crossed = lax.ppermute(low_sum(kept1[1], traded[2]), "ctx", CHIP_SWAP)
     got = plane_swap(send, 0)
     late_keep, late_send, grad_qkv = projection_grads(
@@ -1327,8 +1356,7 @@
     grad_inputs, grad_inputs_1, gain_one_grad = input_grads(
         grad_qkv, w_qkv, x0, x1, grad_state, gain_columns, late_keep
     )
-    early = tied_sum((keep[0], got[0]), gain_one_grad)
-    late_keep, late_send = late_halves(late_keep, late_got, early)
+    early, late_keep, late_send = finish_early(keep, got, late_keep, late_got, gain_one_grad)
     gain_grad = jnp.concatenate([gain_one_grad[:, 0].reshape(1, D), gain_two_grad], axis=0)
     gain_grad = gain_grad + sum(
         lax.ppermute(gain_grad, "ctx", [(place, place ^ turn) for place in range(4)])

time: 386 us -> 381 us (0.987)
  Pallas kernels: 204 us -> 200 us
    pallas_call x10 -> x7, Pallas kernels: 25.5 us -> 16.2 us  [plain_call(): pl.pallas_call(run, out_shape=outs, in_specs=[vmem()] * count + [anywhere...]
    pallas_call x2, Pallas kernels: 3.65 us -> 8.62 us  [early_halves(): pl.pallas_call(kernel, out_shape=[half, half] + [jax.ShapeDtypeStruct(one...]
    unnamed x101 -> x99, local copies, waits for them, and re-layouts: 14.1 us -> 14.1 us
  transfers between devices with their start and end apart: 40 -> 40, of which waited for: 18 -> 17; matrix products, arithmetic and copies ran while one was open for 3% -> 3% of each run, Pallas kernels for 38% -> 38%
where the time goes in v1:
time: 381 us; the launch traced here: 374 us
  Pallas kernels  200 us (52%)
  waiting for transfers between devices  99.9 us (26%)
  starting transfers between devices  33 us (9%)
  local copies, waits for them, and re-layouts  18.8 us (5%)
  between operations  14.6 us (4%)
  other arithmetic  8.15 us (2%)
    pallas_call x2, Pallas kernels, attend_back(): pl.pallas_call(partial(backward_kernel, micro), out_shape=(jax.ShapeDtype...  46 us
    ppermute x13, waiting for transfers between devices, plane_swap(): return lax.ppermute(value, axis, swap)  43.5 us
    pallas_call x1, Pallas kernels, mlp(): pl.pallas_call(mlp_kernel, out_shape=(jax.ShapeDtypeStruct((2, D, TOK), j...  39 us
    pallas_call x2, Pallas kernels, attend_forward(): pl.pallas_call(partial(forward_kernel, micro), out_shape=(jax.ShapeDtypeS...  34.3 us
    pallas_call x1, Pallas kernels, newton(): pl.pallas_call(partial(newton_kernel, local, length), out_shape=outs, in_...  27.1 us
    pallas_call x7, Pallas kernels, plain_call(): pl.pallas_call(run, out_shape=outs, in_specs=[vmem()] * count + [anywhere...  16.2 us
    unnamed x99, local copies, waits for them, and re-layouts  14.1 us
    ppermute x1, waiting for transfers between devices, per_device(): far = lax.ppermute(keyvals[0], 'ctx', CHIP_SWAP)  13.2 us
  transfers between devices with their start and end apart: 40, of which 17 were waited for; matrix products, arithmetic and copies ran while one was open for 3% of the time, Pallas kernels for 38%

profile of v1, /device:TPU:8, one launch (start us, length us, event | category | flops | bytes accessed | tf_op | source)
XLA Modules:
  0.0 374.0 jit_solution(598023580545104396)
XLA Ops:
  7.2 1.1 slice_bitcast_fusion.1
  8.3 1.0 collective-permute-start
  9.3 1.0 bitcast_convert_fusion.refs_0_
  10.4 1.4 collective-permute-start.1
  13.2 3.5 collective-permute-start.11
  16.7 4.0 %collective-permute-done.1.refs_1_ = bf16[864,128]{1,0:T(8,128)(2,1)S(1)} collective-permute-done((bf16[864,128]{1,0:T(8,128)(2,1)S(1)}, bf16[864,128]{1,0:T(8,128)(2,1)S(1)}, u32[]{:S(2)}, u32[]{:S(2)}) %collective-permute-start.1) | collective-permute-done | bytes 221216 | tf_op jit(solution)/shard_map/ppermute | solution.py:1237
  20.7 3.4 collective-permute-start.12
  24.1 2.8 collective-permute-start.13
  28.5 2.0 pick_first.1.refs_4_
  30.5 1.5 collective-permute-done.11.refs_1_
  32.0 4.4 %collective-permute-done.12.refs_2_ = bf16[864,128]{1,0:T(8,128)(2,1)S(1)} collective-permute-done((bf16[864,128]{1,0:T(8,128)(2,1)S(1)}, bf16[864,128]{1,0:T(8,128)(2,1)S(1)}, u32[]{:S(2)}, u32[]{:S(2)}) %collective-permute-start.12) | collective-permute-done | bytes 221216 | tf_op jit(solution)/shard_map/ppermute | solution.py:1240
  36.4 5.7 %collective-permute-done.13.refs_3_ = bf16[864,128]{1,0:T(8,128)(2,1)S(1)} collective-permute-done((bf16[864,128]{1,0:T(8,128)(2,1)S(1)}, bf16[864,128]{1,0:T(8,128)(2,1)S(1)}, u32[]{:S(2)}, u32[]{:S(2)}) %collective-permute-start.13) | collective-permute-done | bytes 221216 | tf_op jit(solution)/shard_map/ppermute | solution.py:1240
  42.8 2.4 pick_rest.1
  46.9 6.5 %collective-permute-done.4 = bf16[1,864,128]{2,1,0:T(8,128)(2,1)S(1)} collective-permute-done((bf16[1,864,128]{2,1,0:T(8,128)(2,1)S(1)}, bf16[1,864,128]{2,1,0:T(8,128)(2,1)S(1)}, u32[]{:S(2)}, u32[]{:S(2)}) %collective-permute-start.4) | collective-permute-done | bytes 221216 | tf_op jit(solution)/shard_map/ppermute | solution.py:1199
  53.5 1.6 collective-permute-start.5
  55.1 10.5 %collective-permute-done.5 = bf16[2,864,128]{2,1,0:T(8,128)(2,1)S(1)} collective-permute-done((bf16[2,864,128]{2,1,0:T(8,128)(2,1)S(1)}, bf16[2,864,128]{2,1,0:T(8,128)(2,1)S(1)}, u32[]{:S(2)}, u32[]{:S(2)}) %collective-permute-start.5) | collective-permute-done | bytes 442400 | tf_op jit(solution)/shard_map/ppermute | solution.py:1199
  65.9 0.9 copy.20
  66.8 1.2 multiply_sine_fusion
  68.0 1.1 broadcast_select_fusion
  69.2 7.8 %project.1 = (bf16[3,3,64,512]{3,2,1,0:T(8,128)(2,1)}, bf16[3,3,64,512]{3,2,1,0:T(8,128)(2,1)}, bf16[2,384,512]{2,1,0:T(8,128)(2,1)}, bf16[576,960]{1,0:T(8,128)...) custom-call(bf16[4,864,128]{2,1,0:T(8,128)(2,1)} %copy-done.11, ...), custom_call_target="tpu_custom_call" | custom-call | flops 1132462080 | bytes 8000000 | tf_op jit(solution)/shard_map/project/pallas_call | solution.py:620
  76.9 1.0 slice_bitcast_fusion.3
  77.9 1.5 collective-permute-start.9
  79.7 13.2 %collective-permute-done.9.far_ref = bf16[384,512]{1,0:T(8,128)(2,1)S(1)} collective-permute-done((bf16[384,512]{1,0:T(8,128)(2,1)S(1)}, bf16[384,512]{1,0:T(8,128)(2,1)S(1)}, u32[]{:S(2)}, u32[]{:S(2)}) %collective-permute-start.9) | collective-permute-done | bytes 393248 | tf_op jit(solution)/shard_map/ppermute | solution.py:1282
  92.9 0.9 slice_bitcast_fusion.refs_1_
  93.8 2.1 low_copies.1
  95.9 2.5 collective-permute-start.7
  100.0 25.3 %attend_forward.3 = (bf16[3,3,64,512]{3,2,1,0:T(8,128)(2,1)}, f32[3,3,1,512]{3,2,1,0:T(1,128)}) custom-call(s32[2,4]{1,0:T(2,128)} %bitcast.74, bf16[3,3,64,512]{3,2,1,0:T(8,128)(2,1)} %get-tuple-element.60.refs_2_.q_ref, bf16[2,384,512]{2,1,0:T(8,128)(2,1)} %get-tuple-element.63.kv_ref, bf16[2,384,512]{2,1,0:T(8,128)(2,1)} %copy-done.42, ...), custom_call_target="tpu_custom_call" | custom-call | flops 2415919104 | bytes 4000000 | tf_op jit(solution)/shard_map/attend_forward/pallas_call | solution.py:341
  125.4 8.9 %attend_forward.2 = (bf16[3,3,64,512]{3,2,1,0:T(8,128)(2,1)}, f32[3,3,1,512]{3,2,1,0:T(1,128)}) custom-call(s32[2,4]{1,0:T(2,128)} %bitcast.75, bf16[3,3,64,512]{3,2,1,0:T(8,128)(2,1)} %get-tuple-element.62.q_ref, bf16[2,384,512]{2,1,0:T(8,128)(2,1)} %get-tuple-element.63.kv_ref, bf16[2,384,512]{2,1,0:T(8,128)(2,1)} %copy-done.42, ...), custom_call_target="tpu_custom_call" | custom-call | flops 2415919104 | bytes 4000000 | tf_op jit(solution)/shard_map/attend_forward/pallas_call | solution.py:341
  135.1 39.0 %mlp.1 = (f32[2,576,512]{2,1,0:T(8,128)}, bf16[576,512]{1,0:T(8,128)(2,1)}, f32[2,576,512]{2,1,0:T(8,128)}, bf16[576,512]{1,0:T(8,128)(2,1)}, bf16[576,512]{1,0:...) custom-call(bf16[576,512]{1,0:T(8,128)(2,1)} %get-tuple-element.116., ...), custom_call_target="tpu_custom_call" | custom-call | flops 16307453952 | bytes 25000000 | tf_op jit(solution)/shard_map/mlp/pallas_call | solution.py:511
  174.1 10.6 %attend_back.2 = (bf16[3,3,64,512]{3,2,1,0:T(8,128)(2,1)}, bf16[1,384,512]{2,1,0:T(8,128)(2,1)}, bf16[1,384,512]{2,1,0:T(8,128)(2,1)}) custom-call(s32[2,4]{1,0:T(2,128)} %bitcast.76, bf16[3,3,64,512]{3,2,1,0:T(8,128)(2,1)} %get-tuple-element.62.q_ref, bf16[2,384,512]{2,1,0:T(8,128)(2,1)} %get-tuple-element.63.kv_ref, bf16[2,384,512]{2,1,0:T(8,128)(2,1)} %copy-done.42, ...), custom_call_target="tpu_custom_call" | custom-call | flops 6039797760 | bytes 8000000 | tf_op jit(solution)/shard_map/attend_back/pallas_call | solution.py:368
  184.7 1.5 copy-done.1
  186.2 5.0 %early_halves.2 = (bf16[2,3,144,768]{3,2,1,0:T(8,128)(2,1)}, bf16[2,3,144,768]{3,2,1,0:T(8,128)(2,1)}) custom-call(bf16[4,3,144,768]{3,2,1,0:T(8,128)(2,1)} %get-tuple-element.79.keep_ref, bf16[4,3,144,768]{3,2,1,0:T(8,128)(2,1)} %copy-done.1, bf16[3,3,64,512]{3,2,1,0:T(8,128)(2,1)} %get-tuple-element.75.refs_0_), custom_call_target="tpu_custom_call" | custom-call | tf_op jit(solution)/shard_map/early_halves/pallas_call | solution.py:778
  191.3 35.4 %attend_back.3 = (bf16[3,3,64,512]{3,2,1,0:T(8,128)(2,1)}, bf16[2,384,512]{2,1,0:T(8,128)(2,1)}, bf16[3,384,512]{2,1,0:T(8,128)(2,1)}) custom-call(s32[2,4]{1,0:T(2,128)} %bitcast.77, bf16[3,3,64,512]{3,2,1,0:T(8,128)(2,1)} %get-tuple-element.60.refs_2_.q_ref, bf16[2,384,512]{2,1,0:T(8,128)(2,1)} %get-tuple-element.63.kv_ref, ...), custom_call_target="tpu_custom_call" | custom-call | flops 6039797760 | bytes 8000000 | tf_op jit(solution)/shard_map/attend_back/pallas_call | solution.py:368
  228.0 3.6 early_halves.3
  231.6 3.1 collective-permute-done.17.got_ref
  235.1 10.8 %collective-permute-done.18.far_ref = bf16[384,512]{1,0:T(8,128)(2,1)S(1)} collective-permute-done((bf16[384,512]{1,0:T(8,128)(2,1)S(1)}, bf16[384,512]{1,0:T(8,128)(2,1)S(1)}, u32[]{:S(2)}, u32[]{:S(2)}) %collective-permute-start.18) | collective-permute-done | bytes 393248 | tf_op jit(solution)/shard_map/ppermute | solution.py:1341
  246.7 7.0 %projection_grads.1 = (bf16[4,144,768]{2,1,0:T(8,128)(2,1)}, bf16[4,144,768]{2,1,0:T(8,128)(2,1)}, bf16[960,1024]{1,0:T(8,128)(2,1)}) custom-call(bf16[576,1024]{1,0:T(8,128)(2,1)} %get-tuple-element.72.n_ref, bf16[576,512]{1,0:T(8,128)(2,1)} %bitcast.54, bf16[576,512]{1,0:T(8,128)(2,1)} %bitcast.63, bf16[1,384,512]{2,1,0:T(8,128)(2,1)} %get-tuple-element.83.kept0_ref, ...), custom_call_target="tpu_custom_call" | custom-call | flops 1132462080 | bytes 8000000 | tf_op jit(solution)/shard_map/projection_grads/pallas_call | solution.py:682
  254.1 2.2 collective-permute-done.19.refs_1_
  256.3 0.9 copy-done.13
  257.2 2.4 late_halves.1
  259.7 2.2 collective-permute-start.22
  261.9 7.6 %input_grads.1 = (f32[2,576,512]{2,1,0:T(8,128)}, bf16[576,512]{1,0:T(8,128)(2,1)}, f32[576,128]{1,0:T(8,128)}) custom-call(bf16[960,1024]{1,0:T(8,128)(2,1)} %get-tuple-element.90.all_ref, bf16[576,960]{1,0:T(8,128)(2,1)} %get-tuple-element.91.w_ref, bf16[576,512]{1,0:T(8,128)(2,1)} %get-tuple-element.116.x_ref, ...), custom_call_target="tpu_custom_call" | custom-call | flops 1132462080 | bytes 8000000 | tf_op jit(solution)/shard_map/input_grads/pallas_call | solution.py:876
  269.5 1.1 slice_reduce_fusion
  270.8 1.8 collective-permute-start.25
  274.3 2.7 finish_early.1
  277.0 1.7 collective-permute-start.23
  278.9 1.9 collective-permute-start.32
  280.9 4.0 %collective-permute-done.23.refs_1_ = bf16[1,144,768]{2,1,0:T(8,128)(2,1)S(1)} collective-permute-done((bf16[1,144,768]{2,1,0:T(8,128)(2,1)}, bf16[1,144,768]{2,1,0:T(8,128)(2,1)S(1)}, u32[]{:S(2)}, u32[]{:S(2)}) %collective-permute-start.23) | collective-permute-done | bytes 221216 | tf_op jit(solution)/shard_map/ppermute | solution.py:1199
  285.6 2.4 depth_turns.1
  288.7 1.2 collective-permute-start.29
  290.0 1.3 add_add_fusion.refs_5_
  291.3 3.8 %lay_momentum.1.refs_4_.refs_2_ = f32[576,1536]{1,0:T(8,128)} custom-call(bf16[6912,128]{1,0:T(8,128)(2,1)} %all-gather.8.cloned.1.call-done.refs_1_.old_ref, bf16[144,768]{1,0:T(8,128)(2,1)} %get-tuple-element.105.tie_ref.refs_0_), custom_call_target="tpu_custom_call" | custom-call | tf_op jit(solution)/shard_map/lay_momentum/pallas_call | solution.py:1086
  295.1 1.4 collective-permute-done.27.refs_1_
  296.5 10.6 %collective-permute-done.28.refs_2_ = bf16[144,768]{1,0:T(8,128)(2,1)S(1)} collective-permute-done((bf16[144,768]{1,0:T(8,128)(2,1)}, bf16[144,768]{1,0:T(8,128)(2,1)S(1)}, u32[]{:S(2)}, u32[]{:S(2)}) %collective-permute-start.28) | collective-permute-done | bytes 221216 | tf_op jit(solution)/shard_map/ppermute | solution.py:1222
  308.7 2.2 tied_sum.1
  310.9 1.6 collective-permute-start.33
  312.5 6.0 %collective-permute-done.33 = bf16[1,144,768]{2,1,0:T(8,128)(2,1)S(1)} collective-permute-done((bf16[1,144,768]{2,1,0:T(8,128)(2,1)}, bf16[1,144,768]{2,1,0:T(8,128)(2,1)S(1)}, u32[]{:S(2)}, u32[]{:S(2)}) %collective-permute-start.33) | collective-permute-done | bytes 221216 | tf_op jit(solution)/shard_map/ppermute | solution.py:1199
  318.5 1.0 pad_maximum_fusion.3
  319.7 11.1 %collective-permute-done.34 = bf16[2,144,768]{2,1,0:T(8,128)(2,1)S(1)} collective-permute-done((bf16[2,144,768]{2,1,0:T(8,128)(2,1)S(1)}, bf16[2,144,768]{2,1,0:T(8,128)(2,1)S(1)}, u32[]{:S(2)}, u32[]{:S(2)}) %collective-permute-start.34) | collective-permute-done | bytes 442400 | tf_op jit(solution)/shard_map/ppermute | solution.py:1199
  330.8 1.0 pad_maximum_fusion.1.refs_0_
  332.6 3.1 collective-permute-done.36
  336.3 0.9 copy-done.41
  337.2 27.1 %newton.1 = (f32[864,128]{1,0:T(8,128)}, f32[864,128]{1,0:T(8,128)}, f32[864,128]{1,0:T(8,128)}) custom-call(bf16[4,144,768]{2,1,0:T(8,128)(2,1)} %copy-done.12, bf16[4,144,768]{2,1,0:T(8,128)(2,1)} %copy-done.41, f32[576,1536]{1,0:T(8,128)} %lay_momentum.1.refs_4_.refs_2_, f32[864,128]{1,0:T(8,128)} %bitcast.67, f32[864,128]{1,0:T(8,128)} %bitcast.66), custom_call_target="tpu_custom_call" | custom-call | flops 12000000000 | bytes 9000000 | tf_op jit(solution)/shard_map/newton/pallas_call | solution.py:1144
  365.1 2.2 place_last.1
  (167 shorter events, 18.5 us)
Async XLA Ops:
  7.2 127.2 %all-gather.6.cloned.1.call-start = ((), (), s32[]{:S(2)}) async-start(), calls=%async_computation.1 | async-start | bytes 2211840 | tf_op jit(solution)/shard_map/all_gather | solution.py:1244
  8.3 18.7 %collective-permute-start = (bf16[576,512]{1,0:T(8,128)(2,1)S(1)}, bf16[576,512]{1,0:T(8,128)(2,1)S(1)}, u32[]{:S(2)}, u32[]{:S(2)}) collective-permute-start(bf16[576,512]{1,0:T(8,128)(2,1)S(1)} %slice_bitcast_fusion.1), channel_id=1, source_target_pairs={{0,3},{3,0},{1,2},{2,1},{4,7},{7,4},{5,6},{6,5},{8,11},{11,8},{9,1... | collective-permute-start | bytes 1769480 | tf_op jit(solution)/shard_map/ppermute | solution.py:1261
  10.4 16.6 %copy-start.7 = (bf16[864,128]{1,0:T(8,128)(2,1)}, bf16[864,128]{1,0:T(8,128)(2,1)S(1)}, u32[]{:S(2)}) copy-start(bf16[864,128]{1,0:T(8,128)(2,1)S(1)} %bitcast_convert_fusion.refs_0_) | copy-start | bytes 663556
  10.4 36.2 %copy-start.38 = (s32[2,1,4]{2,1,0:T(1,128)S(1)}, s32[2,1,4]{2,1,0:T(1,128)}, u32[]{:S(2)}) copy-start(s32[2,1,4]{2,1,0:T(1,128)} %param.9) | copy-start | bytes 100
  10.4 10.3 %collective-permute-start.1 = (bf16[864,128]{1,0:T(8,128)(2,1)S(1)}, bf16[864,128]{1,0:T(8,128)(2,1)S(1)}, u32[]{:S(2)}, u32[]{:S(2)}) collective-permute-start(bf16[864,128]{1,0:T(8,128)(2,1)S(1)} %bitcast_convert_fusion.refs_0_), channel_id=1, source_target_pairs={{0,8},{1,9},{2,10},{3,11},{4,12},{5,13},{6,14},{7,15}} | collective-permute-start | bytes 663560 | tf_op jit(solution)/shard_map/ppermute | solution.py:1237
  11.8 12.3 %collective-permute-start.2 = (bf16[864,128]{1,0:T(8,128)(2,1)S(1)}, bf16[864,128]{1,0:T(8,128)(2,1)S(1)}, u32[]{:S(2)}, u32[]{:S(2)}) collective-permute-start(bf16[864,128]{1,0:T(8,128)(2,1)S(1)} %bitcast_convert_fusion.refs_0_), channel_id=1, source_target_pairs={{0,16},{1,17},{2,18},{3,19},{4,20},{5,21},{6,22},{7,23}} | collective-permute-start | bytes 663560 | tf_op jit(solution)/shard_map/ppermute | solution.py:1237
  12.5 14.5 %collective-permute-start.3 = (bf16[864,128]{1,0:T(8,128)(2,1)S(1)}, bf16[864,128]{1,0:T(8,128)(2,1)S(1)}, u32[]{:S(2)}, u32[]{:S(2)}) collective-permute-start(bf16[864,128]{1,0:T(8,128)(2,1)S(1)} %bitcast_convert_fusion.refs_0_), channel_id=1, source_target_pairs={{0,24},{1,25},{2,26},{3,27},{4,28},{5,29},{6,30},{7,31}} | collective-permute-start | bytes 663560 | tf_op jit(solution)/shard_map/ppermute | solution.py:1237
  13.2 18.8 %collective-permute-start.11 = (bf16[864,128]{1,0:T(8,128)(2,1)S(1)}, bf16[864,128]{1,0:T(8,128)(2,1)S(1)}, u32[]{:S(2)}, u32[]{:S(2)}) collective-permute-start(bf16[864,128]{1,0:T(8,128)(2,1)S(1)} %bitcast_convert_fusion.refs_0_), channel_id=1, source_target_pairs={{8,16},{16,24},{24,0},{9,17},{17,25},{25,1},{10,18},{18,26},{26,2}... | collective-permute-start | bytes 663560 | tf_op jit(solution)/shard_map/ppermute | solution.py:1240
  20.7 6.3 %copy-start.20 = (bf16[864,128]{1,0:T(8,128)(2,1)}, bf16[864,128]{1,0:T(8,128)(2,1)S(1)}, u32[]{:S(2)}) copy-start(bf16[864,128]{1,0:T(8,128)(2,1)S(1)} %collective-permute-done.1.refs_1_) | copy-start | bytes 663556
  20.7 15.7 %collective-permute-start.12 = (bf16[864,128]{1,0:T(8,128)(2,1)S(1)}, bf16[864,128]{1,0:T(8,128)(2,1)S(1)}, u32[]{:S(2)}, u32[]{:S(2)}) collective-permute-start(bf16[864,128]{1,0:T(8,128)(2,1)S(1)} %bitcast_convert_fusion.refs_0_), channel_id=1, source_target_pairs={{8,24},{16,0},{24,8},{9,25},{17,1},{25,9},{10,26},{18,2},{26,10},{... | collective-permute-start | bytes 663560 | tf_op jit(solution)/shard_map/ppermute | solution.py:1240
  24.1 18.0 %collective-permute-start.13 = (bf16[864,128]{1,0:T(8,128)(2,1)S(1)}, bf16[864,128]{1,0:T(8,128)(2,1)S(1)}, u32[]{:S(2)}, u32[]{:S(2)}) collective-permute-start(bf16[864,128]{1,0:T(8,128)(2,1)S(1)} %bitcast_convert_fusion.refs_0_), channel_id=1, source_target_pairs={{8,0},{16,8},{24,16},{9,1},{17,9},{25,17},{10,2},{18,10},{26,18},{... | collective-permute-start | bytes 663560 | tf_op jit(solution)/shard_map/ppermute | solution.py:1240
  30.5 15.5 %copy-start = (bf16[864,128]{1,0:T(8,128)(2,1)S(1)}, bf16[864,128]{1,0:T(8,128)(2,1)}, u32[]{:S(2)}) copy-start(bf16[864,128]{1,0:T(8,128)(2,1)} %pick_first.1.refs_4_) | copy-start | bytes 663556
  32.0 10.1 %copy-start.24 = (bf16[864,128]{1,0:T(8,128)(2,1)}, bf16[864,128]{1,0:T(8,128)(2,1)S(1)}, u32[]{:S(2)}) copy-start(bf16[864,128]{1,0:T(8,128)(2,1)S(1)} %collective-permute-done.11.refs_1_) | copy-start | bytes 663556
  45.1 20.7 %copy-start.29 = (f32[2,576]{1,0:T(2,128)S(1)}, f32[2,576]{1,0:T(2,128)}, u32[]{:S(2)}) copy-start(f32[2,576]{1,0:T(2,128)} %refs_2_.1) | copy-start | bytes 13828
  45.2 89.2 %all-gather.4.cloned.1.call-start = ((), (), s32[]{:S(2)}) async-start(), calls=%async_computation | async-start | bytes 3981312 | tf_op jit(solution)/shard_map/all_gather | solution.py:1244
  45.2 22.8 %copy-start.5 = (bf16[576,512]{1,0:T(8,128)(2,1)S(1)}, bf16[576,512]{1,0:T(8,128)(2,1)}, u32[]{:S(2)}) copy-start(bf16[576,512]{1,0:T(8,128)(2,1)} %copy-done.4) | copy-start | bytes 1769476
  45.2 22.8 %copy-start.10 = (bf16[2,512,576]{1,2,0:T(8,128)(2,1)S(1)}, bf16[2,512,576]{1,2,0:T(8,128)(2,1)}, u32[]{:S(2)}) copy-start(bf16[2,512,576]{1,2,0:T(8,128)(2,1)} %param.8) | copy-start | bytes 3538948
  45.9 180.8 %all-gather.8.cloned.1.call-start = ((), (), s32[]{:S(2)}) async-start(), calls=%async_computation.2 | async-start | bytes 1990656 | tf_op jit(solution)/shard_map/all_gather | solution.py:1298
  46.0 7.4 %collective-permute-start.4 = (bf16[1,864,128]{2,1,0:T(8,128)(2,1)S(1)}, bf16[1,864,128]{2,1,0:T(8,128)(2,1)S(1)}, u32[]{:S(2)}, u32[]{:S(2)}) collective-permute-start(bf16[1,864,128]{2,1,0:T(8,128)(2,1)S(1)} %bitcast.51), channel_id=1, source_target_pairs={{0,2},{2,0},{1,3},{3,1},{4,6},{6,4},{5,7},{7,5},{8,10},{10,8},{9,1... | collective-permute-start | bytes 663560 | tf_op jit(solution)/shard_map/ppermute | solution.py:1199
  53.5 12.2 %collective-permute-start.5 = (bf16[2,864,128]{2,1,0:T(8,128)(2,1)S(1)}, bf16[2,864,128]{2,1,0:T(8,128)(2,1)S(1)}, u32[]{:S(2)}, u32[]{:S(2)}) collective-permute-start(bf16[2,864,128]{2,1,0:T(8,128)(2,1)S(1)} %pad_maximum_fusion.2), channel_id=1, source_target_pairs={{0,4},{4,0},{1,5},{5,1},{2,6},{6,2},{3,7},{7,3},{8,12},{12,8},{9,1... | collective-permute-start | bytes 1327112 | tf_op jit(solution)/shard_map/ppermute | solution.py:1199
  55.1 14.0 %copy-start.34 = (s32[512]{0:T(512)}, s32[512]{0:T(512)S(1)}, u32[]{:S(2)}) copy-start(s32[512]{0:T(512)S(1)} %get-tuple-element.127) | copy-start | bytes 6148
  55.1 14.0 %copy-start.35 = (s32[512]{0:T(512)}, s32[512]{0:T(512)S(1)}, u32[]{:S(2)}) copy-start(s32[512]{0:T(512)S(1)} %get-tuple-element.128) | copy-start | bytes 6148
  65.8 3.3 collective-permute-start.6
  69.1 23.7 %copy-start.18 = (bf16[2,512,576]{1,2,0:T(8,128)(2,1)S(1)}, bf16[2,512,576]{1,2,0:T(8,128)(2,1)}, u32[]{:S(2)}) copy-start(bf16[2,512,576]{1,2,0:T(8,128)(2,1)} %param.15) | copy-start | bytes 3538948
  77.9 14.9 %collective-permute-start.9 = (bf16[384,512]{1,0:T(8,128)(2,1)S(1)}, bf16[384,512]{1,0:T(8,128)(2,1)S(1)}, u32[]{:S(2)}, u32[]{:S(2)}) collective-permute-start(bf16[384,512]{1,0:T(8,128)(2,1)S(1)} %slice_bitcast_fusion.3), channel_id=1, source_target_pairs={{0,2},{2,0},{1,3},{3,1},{4,6},{6,4},{5,7},{7,5},{8,10},{10,8},{9,1... | collective-permute-start | bytes 1179656 | tf_op jit(solution)/shard_map/ppermute | solution.py:1282
  79.5 19.5 %collective-permute-start.8 = (bf16[2,384,512]{2,1,0:T(8,128)(2,1)}, bf16[2,384,512]{2,1,0:T(8,128)(2,1)S(1)}, u32[]{:S(2)}, u32[]{:S(2)}) collective-permute-start(bf16[2,384,512]{2,1,0:T(8,128)(2,1)} %get-tuple-element.63.kv_ref), channel_id=1, source_target_pairs={{0,1},{1,0},{2,3},{3,2},{4,5},{5,4},{6,7},{7,6},{8,9},{9,8},{10,11... | collective-permute-start | bytes 2359304 | tf_op jit(solution)/shard_map/ppermute | solution.py:1285
  92.9 6.1 %collective-permute-start.10 = (bf16[384,512]{1,0:T(8,128)(2,1)S(1)}, bf16[384,512]{1,0:T(8,128)(2,1)S(1)}, u32[]{:S(2)}, u32[]{:S(2)}) collective-permute-start(bf16[384,512]{1,0:T(8,128)(2,1)S(1)} %collective-permute-done.9.far_ref), channel_id=1, source_target_pairs={{0,1},{1,0},{2,3},{3,2},{4,5},{5,4},{6,7},{7,6},{8,9},{9,8},{10,11... | collective-permute-start | bytes 1179656 | tf_op jit(solution)/shard_map/ppermute | solution.py:1287
  95.9 38.4 %collective-permute-start.7 = (bf16[576,512]{1,0:T(8,128)(2,1)}, bf16[576,512]{1,0:T(8,128)(2,1)S(1)}, u32[]{:S(2)}, u32[]{:S(2)}) collective-permute-start(bf16[576,512]{1,0:T(8,128)(2,1)} %get-tuple-element.61), channel_id=1, source_target_pairs={{0,3},{3,0},{1,2},{2,1},{4,7},{7,4},{5,6},{6,5},{8,11},{11,8},{9,1... | collective-permute-start | bytes 1769480 | tf_op jit(solution)/shard_map/ppermute | solution.py:1297
  174.1 10.6 %collective-permute-start.15 = (bf16[4,3,144,768]{3,2,1,0:T(8,128)(2,1)}, bf16[4,3,144,768]{3,2,1,0:T(8,128)(2,1)S(1)}, u32[]{:S(2)}, u32[]{:S(2)}) collective-permute-start(bf16[4,3,144,768]{3,2,1,0:T(8,128)(2,1)} %get-tuple-element.80), channel_id=1, source_target_pairs={{0,1},{1,0},{2,3},{3,2},{4,5},{5,4},{6,7},{7,6},{8,9},{9,8},{10,11... | collective-permute-start | bytes 7962632 | tf_op jit(solution)/shard_map/ppermute | solution.py:1199
  191.2 35.5 %collective-permute-start.16 = (bf16[2,3,144,768]{3,2,1,0:T(8,128)(2,1)}, bf16[2,3,144,768]{3,2,1,0:T(8,128)(2,1)S(1)}, u32[]{:S(2)}, u32[]{:S(2)}) collective-permute-start(bf16[2,3,144,768]{3,2,1,0:T(8,128)(2,1)} %get-tuple-element.85), channel_id=1, source_target_pairs={{0,4},{4,0},{1,5},{5,1},{2,6},{6,2},{3,7},{7,3},{8,12},{12,8},{9,1... | collective-permute-start | bytes 3981320 | tf_op jit(solution)/shard_map/ppermute | solution.py:1199
  191.2 35.5 %collective-permute-start.14 = (bf16[576,512]{1,0:T(8,128)(2,1)S(1)}, bf16[576,512]{1,0:T(8,128)(2,1)S(1)}, u32[]{:S(2)}, u32[]{:S(2)}) collective-permute-start(bf16[576,512]{1,0:T(8,128)(2,1)S(1)} %copy-done.45), channel_id=1, source_target_pairs={{0,3},{3,0},{1,2},{2,1},{4,7},{7,4},{5,6},{6,5},{8,11},{11,8},{9,1... | collective-permute-start | bytes 1769480 | tf_op jit(solution)/shard_map/ppermute | solution.py:1317
  228.0 6.7 %copy-start.8 = (bf16[2,384,512]{2,1,0:T(8,128)(2,1)S(1)}, bf16[2,384,512]{2,1,0:T(8,128)(2,1)}, u32[]{:S(2)}) copy-start(bf16[2,384,512]{2,1,0:T(8,128)(2,1)} %get-tuple-element.84.kept1_ref) | copy-start | bytes 2359300
  231.6 3.1 collective-permute-start.17
  234.7 11.3 %copy-start.6 = (bf16[3,384,512]{2,1,0:T(8,128)(2,1)}, bf16[3,384,512]{2,1,0:T(8,128)(2,1)S(1)}, u32[]{:S(2)}) copy-start(bf16[3,384,512]{2,1,0:T(8,128)(2,1)S(1)} %collective-permute-done.17.got_ref) | copy-start | bytes 3538948
  234.8 11.2 %collective-permute-start.18 = (bf16[384,512]{1,0:T(8,128)(2,1)S(1)}, bf16[384,512]{1,0:T(8,128)(2,1)S(1)}, u32[]{:S(2)}, u32[]{:S(2)}) collective-permute-start(bf16[384,512]{1,0:T(8,128)(2,1)S(1)} %fusion), channel_id=1, source_target_pairs={{0,2},{2,0},{1,3},{3,1},{4,6},{6,4},{5,7},{7,5},{8,10},{10,8},{9,1... | collective-permute-start | bytes 1179656 | tf_op jit(solution)/shard_map/ppermute | solution.py:1341
  246.7 7.0 %copy-start.43 = (bf16[1,3,144,768]{3,2,1,0:T(8,128)(2,1)S(1)}, bf16[1,3,144,768]{3,2,1,0:T(8,128)(2,1)}, u32[]{:S(2)}) copy-start(bf16[1,3,144,768]{3,2,1,0:T(8,128)(2,1)} %get-tuple-element.98) | copy-start | bytes 1990660
  253.7 2.6 collective-permute-start.19
  253.7 19.0 %collective-permute-start.21 = (bf16[1,3,144,768]{3,2,1,0:T(8,128)(2,1)S(1)}, bf16[1,3,144,768]{3,2,1,0:T(8,128)(2,1)S(1)}, u32[]{:S(2)}, u32[]{:S(2)}) collective-permute-start(bf16[1,3,144,768]{3,2,1,0:T(8,128)(2,1)S(1)} %copy-done.43), channel_id=1, source_target_pairs={{0,2},{2,0},{1,3},{3,1},{4,6},{6,4},{5,7},{7,5},{8,10},{10,8},{9,1... | collective-permute-start | bytes 1990664 | tf_op jit(solution)/shard_map/ppermute | solution.py:1199
  259.7 13.0 %collective-permute-start.22 = (bf16[2,144,768]{2,1,0:T(8,128)(2,1)}, bf16[2,144,768]{2,1,0:T(8,128)(2,1)S(1)}, u32[]{:S(2)}, u32[]{:S(2)}) collective-permute-start(bf16[2,144,768]{2,1,0:T(8,128)(2,1)} %get-tuple-element.99), channel_id=1, source_target_pairs={{0,4},{4,0},{1,5},{5,1},{2,6},{6,2},{3,7},{7,3},{8,12},{12,8},{9,1... | collective-permute-start | bytes 1327112 | tf_op jit(solution)/shard_map/ppermute | solution.py:1199
  261.9 8.8 %copy-start.33 = (f32[1,576]{1,0:T(1,128)S(1)}, f32[1,576]{1,0:T(1,128)}, u32[]{:S(2)}) copy-start(f32[1,576]{1,0:T(1,128)} %get-tuple-element.104) | copy-start | bytes 6916
  270.7 8.0 %collective-permute-start.24 = (f32[2,576]{1,0:T(2,128)S(1)}, f32[2,576]{1,0:T(2,128)S(1)}, u32[]{:S(2)}, u32[]{:S(2)}) collective-permute-start(f32[2,576]{1,0:T(2,128)S(1)} %pad_maximum_fusion.4), channel_id=1, source_target_pairs={{0,1},{1,0},{2,3},{3,2},{4,5},{5,4},{6,7},{7,6},{8,9},{9,8},{10,11... | collective-permute-start | bytes 13832 | tf_op jit(solution)/shard_map/ppermute | solution.py:1362
  270.8 7.9 %collective-permute-start.25 = (f32[2,576]{1,0:T(2,128)S(1)}, f32[2,576]{1,0:T(2,128)S(1)}, u32[]{:S(2)}, u32[]{:S(2)}) collective-permute-start(f32[2,576]{1,0:T(2,128)S(1)} %pad_maximum_fusion.4), channel_id=1, source_target_pairs={{0,2},{1,3},{2,0},{3,1},{4,6},{5,7},{6,4},{7,5},{8,10},{9,11},{10,... | collective-permute-start | bytes 13832 | tf_op jit(solution)/shard_map/ppermute | solution.py:1362
  272.6 6.1 %collective-permute-start.26 = (f32[2,576]{1,0:T(2,128)S(1)}, f32[2,576]{1,0:T(2,128)S(1)}, u32[]{:S(2)}, u32[]{:S(2)}) collective-permute-start(f32[2,576]{1,0:T(2,128)S(1)} %pad_maximum_fusion.4), channel_id=1, source_target_pairs={{0,3},{1,2},{2,1},{3,0},{4,7},{5,6},{6,5},{7,4},{8,11},{9,10},{10,... | collective-permute-start | bytes 13832 | tf_op jit(solution)/shard_map/ppermute | solution.py:1362
  277.0 7.9 %collective-permute-start.23 = (bf16[1,144,768]{2,1,0:T(8,128)(2,1)}, bf16[1,144,768]{2,1,0:T(8,128)(2,1)S(1)}, u32[]{:S(2)}, u32[]{:S(2)}) collective-permute-start(bf16[1,144,768]{2,1,0:T(8,128)(2,1)} %get-tuple-element.102), channel_id=1, source_target_pairs={{0,2},{2,0},{1,3},{3,1},{4,6},{6,4},{5,7},{7,5},{8,10},{10,8},{9,1... | collective-permute-start | bytes 663560 | tf_op jit(solution)/shard_map/ppermute | solution.py:1199
  278.8 9.9 %collective-permute-start.30 = (f32[2,576]{1,0:T(2,128)S(1)}, f32[2,576]{1,0:T(2,128)S(1)}, u32[]{:S(2)}, u32[]{:S(2)}) collective-permute-start(f32[2,576]{1,0:T(2,128)S(1)} %add_add_fusion.1.refs_3_), channel_id=1, source_target_pairs={{0,8},{8,16},{16,24},{24,0},{1,9},{9,17},{17,25},{25,1},{2,10},{10... | collective-permute-start | bytes 13832 | tf_op jit(solution)/shard_map/ppermute | solution.py:1222
  278.8 11.1 %collective-permute-start.31 = (f32[2,576]{1,0:T(2,128)S(1)}, f32[2,576]{1,0:T(2,128)S(1)}, u32[]{:S(2)}, u32[]{:S(2)}) collective-permute-start(f32[2,576]{1,0:T(2,128)S(1)} %add_add_fusion.1.refs_3_), channel_id=1, source_target_pairs={{0,16},{8,24},{16,0},{24,8},{1,17},{9,25},{17,1},{25,9},{2,18},{10... | collective-permute-start | bytes 13832 | tf_op jit(solution)/shard_map/ppermute | solution.py:1222
  278.9 11.1 %collective-permute-start.32 = (f32[2,576]{1,0:T(2,128)S(1)}, f32[2,576]{1,0:T(2,128)S(1)}, u32[]{:S(2)}, u32[]{:S(2)}) collective-permute-start(f32[2,576]{1,0:T(2,128)S(1)} %add_add_fusion.1.refs_3_), channel_id=1, source_target_pairs={{0,24},{8,0},{16,8},{24,16},{1,25},{9,1},{17,9},{25,17},{2,26},{10... | collective-permute-start | bytes 13832 | tf_op jit(solution)/shard_map/ppermute | solution.py:1222
  287.9 8.6 %collective-permute-start.27 = (bf16[144,768]{1,0:T(8,128)(2,1)}, bf16[144,768]{1,0:T(8,128)(2,1)S(1)}, u32[]{:S(2)}, u32[]{:S(2)}) collective-permute-start(bf16[144,768]{1,0:T(8,128)(2,1)} %get-tuple-element.106), channel_id=1, source_target_pairs={{0,8},{8,16},{16,24},{24,0},{1,9},{9,17},{17,25},{25,1},{2,10},{10... | collective-permute-start | bytes 663560 | tf_op jit(solution)/shard_map/ppermute | solution.py:1222
  287.9 19.2 %collective-permute-start.28 = (bf16[144,768]{1,0:T(8,128)(2,1)}, bf16[144,768]{1,0:T(8,128)(2,1)S(1)}, u32[]{:S(2)}, u32[]{:S(2)}) collective-permute-start(bf16[144,768]{1,0:T(8,128)(2,1)} %get-tuple-element.107), channel_id=1, source_target_pairs={{0,16},{8,24},{16,0},{24,8},{1,17},{9,25},{17,1},{25,9},{2,18},{10... | collective-permute-start | bytes 663560 | tf_op jit(solution)/shard_map/ppermute | solution.py:1222
  288.7 19.3 %collective-permute-start.29 = (bf16[144,768]{1,0:T(8,128)(2,1)}, bf16[144,768]{1,0:T(8,128)(2,1)S(1)}, u32[]{:S(2)}, u32[]{:S(2)}) collective-permute-start(bf16[144,768]{1,0:T(8,128)(2,1)} %get-tuple-element.108), channel_id=1, source_target_pairs={{0,24},{8,0},{16,8},{24,16},{1,25},{9,1},{17,9},{25,17},{2,26},{10... | collective-permute-start | bytes 663560 | tf_op jit(solution)/shard_map/ppermute | solution.py:1222
  296.5 11.5 %copy-start.23 = (bf16[144,768]{1,0:T(8,128)(2,1)}, bf16[144,768]{1,0:T(8,128)(2,1)S(1)}, u32[]{:S(2)}) copy-start(bf16[144,768]{1,0:T(8,128)(2,1)S(1)} %collective-permute-done.27.refs_1_) | copy-start | bytes 663556
  308.7 23.6 %copy-start.39 = (f32[2,576,512]{2,1,0:T(8,128)S(1)}, f32[2,576,512]{2,1,0:T(8,128)}, u32[]{:S(2)}) copy-start(f32[2,576,512]{2,1,0:T(8,128)} %get-tuple-element.70) | copy-start | bytes 7077892
  310.9 21.0 %copy-start.31 = (f32[2,576]{1,0:T(2,128)S(1)}, f32[2,576]{1,0:T(2,128)}, u32[]{:S(2)}) copy-start(f32[2,576]{1,0:T(2,128)} %add_add_fusion.refs_5_) | copy-start | bytes 13828
  310.9 21.4 %copy-start.3 = (bf16[576,512]{1,0:T(8,128)(2,1)S(1)}, bf16[576,512]{1,0:T(8,128)(2,1)}, u32[]{:S(2)}) copy-start(bf16[576,512]{1,0:T(8,128)(2,1)} %copy-done.2) | copy-start | bytes 1769476
  310.9 7.6 %collective-permute-start.33 = (bf16[1,144,768]{2,1,0:T(8,128)(2,1)}, bf16[1,144,768]{2,1,0:T(8,128)(2,1)S(1)}, u32[]{:S(2)}, u32[]{:S(2)}) collective-permute-start(bf16[1,144,768]{2,1,0:T(8,128)(2,1)} %bitcast.56), channel_id=1, source_target_pairs={{0,2},{2,0},{1,3},{3,1},{4,6},{6,4},{5,7},{7,5},{8,10},{10,8},{9,1... | collective-permute-start | bytes 663560 | tf_op jit(solution)/shard_map/ppermute | solution.py:1199
  319.5 13.0 %copy-start.44 = (bf16[576,512]{1,0:T(8,128)(2,1)S(1)}, bf16[576,512]{1,0:T(8,128)(2,1)}, u32[]{:S(2)}) copy-start(bf16[576,512]{1,0:T(8,128)(2,1)} %get-tuple-element.97) | copy-start | bytes 1769476
  319.5 16.2 %copy-start.30 = (f32[2,576]{1,0:T(2,128)S(1)}, f32[2,576]{1,0:T(2,128)}, u32[]{:S(2)}) copy-start(f32[2,576]{1,0:T(2,128)} %refs_2_.1) | copy-start | bytes 13828
  319.5 16.1 %copy-start.36 = (f32[2,576]{1,0:T(2,128)S(1)}, f32[2,576]{1,0:T(2,128)}, u32[]{:S(2)}) copy-start(f32[2,576]{1,0:T(2,128)} %param.14) | copy-start | bytes 13828
  319.5 16.1 %copy-start.37 = (f32[2,576]{1,0:T(2,128)S(1)}, f32[2,576]{1,0:T(2,128)}, u32[]{:S(2)}) copy-start(f32[2,576]{1,0:T(2,128)} %param.13) | copy-start | bytes 13828
  319.5 11.3 %collective-permute-start.34 = (bf16[2,144,768]{2,1,0:T(8,128)(2,1)S(1)}, bf16[2,144,768]{2,1,0:T(8,128)(2,1)S(1)}, u32[]{:S(2)}, u32[]{:S(2)}) collective-permute-start(bf16[2,144,768]{2,1,0:T(8,128)(2,1)S(1)} %pad_maximum_fusion.3), channel_id=1, source_target_pairs={{0,4},{4,0},{1,5},{5,1},{2,6},{6,2},{3,7},{7,3},{8,12},{12,8},{9,1... | collective-permute-start | bytes 1327112 | tf_op jit(solution)/shard_map/ppermute | solution.py:1199
  331.9 4.4 %collective-permute-start.35 = (bf16[4,144,768]{2,1,0:T(8,128)(2,1)S(1)}, bf16[4,144,768]{2,1,0:T(8,128)(2,1)S(1)}, u32[]{:S(2)}, u32[]{:S(2)}) collective-permute-start(bf16[4,144,768]{2,1,0:T(8,128)(2,1)S(1)} %pad_maximum_fusion.1.refs_0_), channel_id=1, source_target_pairs={{0,1},{1,0},{2,3},{3,2},{4,5},{5,4},{6,7},{7,6},{8,9},{9,8},{10,11... | collective-permute-start | bytes 2654216 | tf_op jit(solution)/shard_map/ppermute | solution.py:1199
  331.9 3.7 collective-permute-start.36
  332.5 31.9 %copy-start.40 = (f32[2,576,512]{2,1,0:T(8,128)}, f32[2,576,512]{2,1,0:T(8,128)S(1)}, u32[]{:S(2)}) copy-start(f32[2,576,512]{2,1,0:T(8,128)S(1)} %convert_dynamic-update-slice_fusion) | copy-start | bytes 7077892
  332.5 31.8 %collective-permute-start.20 = (bf16[576,512]{1,0:T(8,128)(2,1)S(1)}, bf16[576,512]{1,0:T(8,128)(2,1)S(1)}, u32[]{:S(2)}, u32[]{:S(2)}) collective-permute-start(bf16[576,512]{1,0:T(8,128)(2,1)S(1)} %copy-done.44), channel_id=1, source_target_pairs={{0,3},{3,0},{1,2},{2,1},{4,7},{7,4},{5,6},{6,5},{8,11},{11,8},{9,1... | collective-permute-start | bytes 1769480 | tf_op jit(solution)/shard_map/ppermute | solution.py:1375
  (25 other events, 49.3 us)
Sparse Core Ops, SparseCore 0:
  45.3 28.1 all-gather.5
  76.0 45.3 all-gather.3
  174.2 25.1 all-gather.7
